TPU v7x, 128 devices: a whole 4x4x4 slice. The times are simulated.
128 devices in a mesh: gx: 8 (over x, core), gy: 16 (over z, y).
Axes of the slice: x: 4, y: 4, z: 4, core: 2. Of those that a mesh axis runs over, the one named last changes fastest.
Arguments:
- previous_fine_boxes: float32 [1024, 5, 8, 128], P(('gx', 'gy'))
- coarse_state: float32 [5, 128, 8192], P(None, 'gx', 'gy')
- new_source: int32 [1024], replicated, may hold values from 0 to 1023, as said below
- box_position: int32 [1024], replicated, may hold values from 0 to 4095, as said below
Outputs:
- fine_boxes: float32 [1024, 5, 8, 128], P(('gx', 'gy'))
- reflux: float32 [4096, 5, 136], P(('gx', 'gy'))
Inputs may be any that keep to these rules, and one draw needn't show every extreme that they name: `new_source`: a permutation; the old slot of every new slot lies on a device of the same gx index; of the 8 new slots of a device, 4 hold its own old boxes and each other device of its gx group sends it either 0 or exactly 1 boxes. `box_position`: positions of the boxes are distinct; the coarse owner of a box's position lies in the gx group of the box's new owner; the boxes of one new owner lie in either 0 or exactly 2 positions of each coarse device.
All inputs are finite; a program needn't handle non-finite values.
Results may differ from a plain program's by a relative error of at most 0.0003.
Values sent between devices are 32-bit elements; how exact they have to be, the bound alone decides.
A program may use at most 64 MiB of HBM per device.

v0:
```python
from functools import partial

import jax
import jax.numpy as jnp
from jax import lax
from jax.sharding import PartitionSpec as P

PYD = 8
POS_DEV = 32
GHOST_CAP = 2


GAMMA_LESS = 0.4
STEP_RATIO = 0.15
WAVE_SPEED = 2.5


def extended(block, sides, width):
    for axis, dim in sides:
        count = lax.axis_size(axis)
        forward = [(i, i + 1) for i in range(count - 1)]
        forward.append((count - 1, 0))
        backward = [(target, source) for source, target in forward]
        low = lax.ppermute(
            lax.slice_in_dim(block, block.shape[dim] - width, None, axis=dim), axis, forward
        )
        high = lax.ppermute(lax.slice_in_dim(block, 0, width, axis=dim), axis, backward)
        block = jnp.concatenate([low, block, high], axis=dim)
    return block


def minmod(first, second):
    return jnp.where(
        first * second > 0.0, jnp.where(jnp.abs(first) < jnp.abs(second), first, second), 0.0
    )


def physical_flux(state, along_dim):
    inverse = 1.0 / state[0]
    pressure = GAMMA_LESS * (
        state[4] - 0.5 * (state[1] * state[1] + state[2] * state[2] + state[3] * state[3]) * inverse
    )
    normal = state[along_dim] * inverse
    pieces = [
        state[along_dim],
        state[1] * normal,
        state[2] * normal,
        state[3] * normal,
        (state[4] + pressure) * normal,
    ]
    pieces[along_dim] = pieces[along_dim] + pressure
    return jnp.stack(pieces)


def boundary_face_flux(state, along_dim):
    length = state.shape[along_dim]

    def window(start_at, stop_at, source):
        return lax.slice_in_dim(source, start_at, stop_at, axis=along_dim)

    deltas = window(1, length, state) - window(0, length - 1, state)
    limited = minmod(window(0, length - 2, deltas), window(1, length - 1, deltas))
    left_state = window(1, length - 2, state) + 0.5 * window(0, length - 3, limited)
    right_state = window(2, length - 1, state) - 0.5 * window(1, length - 2, limited)
    average = 0.5 * (physical_flux(left_state, along_dim) + physical_flux(right_state, along_dim))
    return average - 0.5 * WAVE_SPEED * (right_state - left_state)


def advance(state):
    x_flux = boundary_face_flux(state, 1)
    y_flux = boundary_face_flux(state, 2)
    inner = state[:, 2:-2, 2:-2]
    result = (
        inner
        - STEP_RATIO * (x_flux[:, 1:, 2:-2] - x_flux[:, :-1, 2:-2])
        - STEP_RATIO * (y_flux[:, 2:-2, 1:] - y_flux[:, 2:-2, :-1])
    )
    return (result, x_flux, y_flux)


def pair_sum(values):
    return values.reshape(values.shape[0], values.shape[1] // 2, 2).sum(axis=2)


def face_sums(x_flux, y_flux, margin, box_rows, box_cols):
    x_lower = x_flux[:, margin - 2, margin : margin + box_cols]
    x_upper = x_flux[:, margin + box_rows - 2, margin : margin + box_cols]
    y_lower = y_flux[:, margin : margin + box_rows, margin - 2]
    y_upper = y_flux[:, margin : margin + box_rows, margin + box_cols - 2]
    return jnp.concatenate(
        [pair_sum(x_lower), pair_sum(x_upper), pair_sum(y_lower), pair_sum(y_upper)], axis=1
    )


def prolong(coarse_block):
    center = coarse_block[:, 1:-1, 1:-1]
    slope_x = minmod(center - coarse_block[:, :-2, 1:-1], coarse_block[:, 2:, 1:-1] - center)
    slope_y = minmod(center - coarse_block[:, 1:-1, :-2], coarse_block[:, 1:-1, 2:] - center)
    offsets = jnp.array([-0.25, 0.25], jnp.float32)
    refined = (
        center[:, :, None, :, None]
        + slope_x[:, :, None, :, None] * offsets[None, None, :, None, None]
        + slope_y[:, :, None, :, None] * offsets[None, None, None, None, :]
    )
    return refined.reshape(coarse_block.shape[0], 2 * center.shape[1], 2 * center.shape[2])


def advance_twice(padded, box_rows, box_cols):
    middle, x_flux, y_flux = advance(padded)
    totals = face_sums(x_flux, y_flux, 4, box_rows, box_cols)
    result, x_flux, y_flux = advance(middle)
    return (result, totals + face_sums(x_flux, y_flux, 2, box_rows, box_cols))


def coarse_faces(coarse_block, half_rows, half_cols):
    x_lower = boundary_face_flux(coarse_block[:, 1:5, 3 : 3 + half_cols], 1)[:, 0]
    x_upper = boundary_face_flux(
        coarse_block[:, half_rows + 1 : half_rows + 5, 3 : 3 + half_cols], 1
    )[:, 0]
    y_lower = boundary_face_flux(coarse_block[:, 3 : 3 + half_rows, 1:5], 2)[:, :, 0]
    y_upper = boundary_face_flux(
        coarse_block[:, 3 : 3 + half_rows, half_cols + 1 : half_cols + 5], 2
    )[:, :, 0]
    return jnp.concatenate([x_lower, x_upper, y_lower, y_upper], axis=1)


def face_signs(half_rows, half_cols):
    return jnp.concatenate(
        [
            jnp.ones((half_cols,), jnp.float32),
            -jnp.ones((half_cols,), jnp.float32),
            jnp.ones((half_rows,), jnp.float32),
            -jnp.ones((half_rows,), jnp.float32),
        ]
    )


def earlier_count(labels):
    order_ids = jnp.arange(labels.shape[1], dtype=jnp.int32)
    before = order_ids[None, :] < order_ids[:, None]
    matching = labels[:, :, None] == labels[:, None, :]
    return jnp.sum(matching & before[None], axis=2)


def local(previous_fine_boxes, coarse_state, new_source, box_position):
    members = lax.axis_size("gy")
    gx_index = lax.axis_index("gx")
    gy_index = lax.axis_index("gy")
    box_count = previous_fine_boxes.shape[0]
    box_rows = previous_fine_boxes.shape[2]
    box_cols = previous_fine_boxes.shape[3]
    half_rows = box_rows // 2
    half_cols = box_cols // 2
    move_cap = max(1, (box_count // 2 + members - 2) // (members - 1))
    coarse_rim = extended(coarse_state, (("gx", 1), ("gy", 2)), 3)
    group_map = lax.dynamic_slice_in_dim(
        new_source, gx_index * members * box_count, members * box_count
    ).reshape(members, box_count)
    peer_ids = jnp.arange(members, dtype=jnp.int32)
    sender_gy = group_map // box_count - gx_index * members
    sender_local = group_map % box_count
    move_rank = earlier_count(sender_gy)
    move_slots = jnp.arange(move_cap, dtype=jnp.int32)
    move_match = (
        (sender_gy[:, None, :] == gy_index)
        & (peer_ids[:, None, None] != gy_index)
        & (move_rank[:, None, :] == move_slots[None, :, None])
    )
    send_local = jnp.sum(jnp.where(move_match, sender_local[:, None, :], 0), axis=2)
    send_live = jnp.any(move_match, axis=2)
    outgoing = jnp.where(send_live[:, :, None, None, None], previous_fine_boxes[send_local], 0.0)
    arriving = lax.all_to_all(outgoing, "gy", split_axis=0, concat_axis=0, tiled=True)
    my_sender = sender_gy[gy_index]
    my_local = sender_local[gy_index]
    my_rank = move_rank[gy_index]
    remaining_boxes = my_sender == gy_index
    arrival_slot = jnp.where(remaining_boxes, 0, my_sender * move_cap + my_rank)
    arrived = arriving.reshape((members * move_cap,) + arriving.shape[2:])[arrival_slot]
    boxes_new = jnp.where(
        remaining_boxes[:, None, None, None], previous_fine_boxes[my_local], arrived
    )
    group_place = box_position[group_map]
    coarse_gy = group_place // POS_DEV - gx_index * members
    coarse_local = group_place % POS_DEV
    ghost_rank = earlier_count(coarse_gy)
    ghost_slots = jnp.arange(GHOST_CAP, dtype=jnp.int32)
    ghost_match = (coarse_gy[:, None, :] == gy_index) & (
        ghost_rank[:, None, :] == ghost_slots[None, :, None]
    )
    ghost_local = jnp.sum(jnp.where(ghost_match, coarse_local[:, None, :], 0), axis=2)
    ghost_live = jnp.any(ghost_match, axis=2)

    def cut_block(local_index):
        zero_index = jnp.zeros((), jnp.int32)
        return lax.dynamic_slice(
            coarse_rim,
            (zero_index, local_index // PYD * half_rows, local_index % PYD * half_cols),
            (5, half_rows + 6, half_cols + 6),
        )

    blocks = jax.vmap(jax.vmap(cut_block))(ghost_local)
    blocks = jnp.where(ghost_live[:, :, None, None, None], blocks, 0.0)
    coarse_terms = STEP_RATIO * jax.vmap(
        jax.vmap(partial(coarse_faces, half_rows=half_rows, half_cols=half_cols))
    )(blocks)
    my_owner = coarse_gy[gy_index]
    my_ghost = ghost_rank[gy_index]
    ghost_pick = my_owner * GHOST_CAP + my_ghost
    received = lax.all_to_all(blocks, "gy", split_axis=0, concat_axis=0, tiled=True)
    chosen = received.reshape((members * GHOST_CAP,) + received.shape[2:])[ghost_pick]
    padded = jax.vmap(prolong)(chosen).at[:, :, 4:-4, 4:-4].set(boxes_new)
    fine_boxes, totals = jax.vmap(partial(advance_twice, box_rows=box_rows, box_cols=box_cols))(
        padded
    )
    box_numbers = jnp.arange(box_count, dtype=jnp.int32)
    back_match = (my_owner[None, None, :] == peer_ids[:, None, None]) & (
        my_ghost[None, None, :] == ghost_slots[None, :, None]
    )
    back_index = jnp.sum(jnp.where(back_match, box_numbers[None, None, :], 0), axis=2)
    back_live = jnp.any(back_match, axis=2)
    returning = jnp.where(back_live[:, :, None, None], totals[back_index], 0.0)
    returned = lax.all_to_all(returning, "gy", split_axis=0, concat_axis=0, tiled=True)
    signs = face_signs(half_rows, half_cols)
    flux_corrections = jnp.where(
        ghost_live[:, :, None, None], signs * (coarse_terms - 0.25 * STEP_RATIO * returned), 0.0
    )
    box_assignment = (
        (ghost_local[:, :, None] == jnp.arange(POS_DEV, dtype=jnp.int32)[None, None, :])
        & ghost_live[:, :, None]
    ).astype(jnp.float32)
    reflux = jnp.einsum(
        "zan,zawk->nwk", box_assignment, flux_corrections, precision=lax.Precision.HIGHEST
    )
    return (fine_boxes, reflux)


def solution(mesh):
    placed = (P(("gx", "gy"), None, None, None), P(None, "gx", "gy"), P(), P())
    return jax.shard_map(
        local,
        mesh=mesh,
        in_specs=placed,
        out_specs=(P(("gx", "gy"), None, None, None), P(("gx", "gy"), None, None)),
        check_vma=False,
    )
```

profile of v0, /device:TPU:0, one launch (start us, length us, event | category | flops | bytes accessed | tf_op | source)
XLA Modules:
  0.0 173.1 jit_solution(16802942360975653055)
XLA Ops:
  1.7 2.9 %collective-permute-start.1 = (f32[5,3,512]{2,1,0:T(4,128)S(1)}, f32[5,3,512]{2,1,0:T(4,128)S(1)}, u32[]{:S(2)}, u32[]{:S(2)}) collective-permute-start(f32[5,3,512]{2,1,0:T(4,128)S(1)} %get-tuple-element.153), channel_id=1, source_target_pairs={{16,0},{32,16},{48,32},{64,48},{80,64},{96,80},{112,96},{0,112},{1... | collective-permute-start | bytes 92168 | tf_op jit(solution)/shard_map/ppermute | solution.py:27
  9.8 8.2 %all-to-all-start.1 = ((f32[16,1,5,8,128]{4,3,2,1,0:T(8,128)}), f32[16,1,5,8,128]{4,3,2,1,0:T(8,128)}, u32[]{:S(2)}, u32[]{:S(2)}) async-start(f32[16,1,5,8,128]{4,3,2,1,0:T(8,128)} %bitcast_select_fusion), calls=%async_computation.1 | async-start | bytes 655360 | tf_op jit(solution)/shard_map/all_to_all | solution.py:172
  21.5 1.9 %collective-permute-start.2 = (f32[5,22,3]{2,1,0:T(8,128)S(1)}, f32[5,22,3]{2,1,0:T(8,128)S(1)}, u32[]{:S(2)}, u32[]{:S(2)}) collective-permute-start(f32[5,22,3]{2,1,0:T(8,128)S(1)} %get-tuple-element.148), channel_id=1, source_target_pairs={{0,1},{1,2},{2,3},{3,4},{4,5},{5,6},{6,7},{7,8},{8,9},{9,10},{10,1... | collective-permute-start | bytes 3968 | tf_op jit(solution)/shard_map/ppermute | solution.py:24
  23.4 3.5 %collective-permute-start.3 = (f32[5,22,3]{2,1,0:T(8,128)S(1)}, f32[5,22,3]{2,1,0:T(8,128)S(1)}, u32[]{:S(2)}, u32[]{:S(2)}) collective-permute-start(f32[5,22,3]{2,1,0:T(8,128)S(1)} %get-tuple-element.149), channel_id=1, source_target_pairs={{1,0},{2,1},{3,2},{4,3},{5,4},{6,5},{7,6},{8,7},{9,8},{10,9},{11,1... | collective-permute-start | bytes 3968 | tf_op jit(solution)/shard_map/ppermute | solution.py:27
  27.7 1.4 collective-permute-done.2
  29.3 63.9 %while.2 = (s32[]{:T(128)}, f32[5,22,518]{2,1,0:T(8,128)S(1)}, s32[32,3]{0,1:T(4,128)S(1)}, f32[32,5,10,70]{3,2,1,0:T(8,128)S(1)}, s32[]{:T(128)}) while((s32[]{:T(128)}, f32[5,22,518]{2,1,0:T(8,128)S(1)}, s32[32,3]{0,1:T(4,128)S(1)}, f32[32,5,10,70]{3,2,1,0:T(8,128)S(1)}, s32[]{:T(128)}) %tuple.107), condition=%wide.while_cond.1, body=%wide.while_body.1.sunk | while | flops 2 | bytes 82045 | solution.py:195
  30.0 1.4 bitcast_dynamic-update-slice_fusion.2
  32.0 1.4 bitcast_dynamic-update-slice_fusion.2
  34.0 1.4 bitcast_dynamic-update-slice_fusion.2
  36.0 1.4 bitcast_dynamic-update-slice_fusion.2
  38.0 1.4 bitcast_dynamic-update-slice_fusion.2
  39.9 1.4 bitcast_dynamic-update-slice_fusion.2
  41.9 1.4 bitcast_dynamic-update-slice_fusion.2
  43.9 1.4 bitcast_dynamic-update-slice_fusion.2
  45.9 1.4 bitcast_dynamic-update-slice_fusion.2
  47.9 1.4 bitcast_dynamic-update-slice_fusion.2
  49.9 1.4 bitcast_dynamic-update-slice_fusion.2
  51.9 1.4 bitcast_dynamic-update-slice_fusion.2
  53.9 1.4 bitcast_dynamic-update-slice_fusion.2
  55.9 1.4 bitcast_dynamic-update-slice_fusion.2
  57.9 1.4 bitcast_dynamic-update-slice_fusion.2
  59.9 1.4 bitcast_dynamic-update-slice_fusion.2
  61.9 1.4 bitcast_dynamic-update-slice_fusion.2
  63.9 1.4 bitcast_dynamic-update-slice_fusion.2
  65.9 1.4 bitcast_dynamic-update-slice_fusion.2
  67.9 1.4 bitcast_dynamic-update-slice_fusion.2
  69.9 1.4 bitcast_dynamic-update-slice_fusion.2
  71.9 1.4 bitcast_dynamic-update-slice_fusion.2
  73.9 1.4 bitcast_dynamic-update-slice_fusion.2
  75.9 1.4 bitcast_dynamic-update-slice_fusion.2
  77.9 1.4 bitcast_dynamic-update-slice_fusion.2
  79.9 1.4 bitcast_dynamic-update-slice_fusion.2
  81.8 1.4 bitcast_dynamic-update-slice_fusion.2
  83.8 1.4 bitcast_dynamic-update-slice_fusion.2
  85.8 1.4 bitcast_dynamic-update-slice_fusion.2
  87.8 1.4 bitcast_dynamic-update-slice_fusion.2
  89.8 1.4 bitcast_dynamic-update-slice_fusion.2
  106.7 1.5 fusion.43
  108.2 6.8 %all-to-all-start = ((f32[16,2,5,10,70]{4,1,3,2,0:T(2,128)}), f32[16,2,5,10,70]{4,1,3,2,0:T(2,128)S(1)}, u32[]{:S(2)}, u32[]{:S(2)}) async-start(f32[16,2,5,10,70]{4,1,3,2,0:T(2,128)} %copy.529), calls=%async_computation | async-start | bytes 1638400 | tf_op jit(solution)/shard_map/all_to_all | solution.py:209
  115.7 1.7 gather_fusion.4
  118.2 8.7 %all-to-all-done = f32[16,2,5,10,70]{4,1,3,2,0:T(2,128)S(1)} async-done(((f32[16,2,5,10,70]{4,1,3,2,0:T(2,128)}), f32[16,2,5,10,70]{4,1,3,2,0:T(2,128)S(1)}, u32[]{:S(2)}, u32[]{:S(2)}) %all-to-all-start) | async-done | bytes 448032 | tf_op jit(solution)/shard_map/all_to_all | solution.py:209
  129.9 1.7 copy.534
  131.6 2.4 %broadcast_multiply_fusion = f32[8,5,8,68,2]{0,4,3,2,1:T(2,128)S(1)} fusion(f32[2]{0:T(128)S(1)} %copy-done.20, f32[8,5,8,68]{0,3,2,1:T(8,128)} %copy.534), kind=kLoop, calls=%fused_computation.10 | loop fusion | flops 43520 | bytes 261128 | tf_op jit(solution)/shard_map/vmap()/mul | solution.py:103
  134.4 4.5 %broadcast_add_fusion = f32[8,5,8,2,68,2]{0,5,4,3,2,1:T(2,128)} fusion(f32[8,5,8,68,2]{0,4,3,2,1:T(2,128)S(1)} %broadcast_multiply_fusion, f32[8,5,8,2,68]{0,4,3,2,1:T(8,128)S(1)} %multiply_add_fusion), kind=kLoop, calls=%fused_computation.9 | loop fusion | flops 87040 | bytes 696320 | tf_op jit(solution)/shard_map/vmap()/add | solution.py:101
  138.9 4.6 %copy.542 = f32[8,5,16,136]{3,0,2,1:T(8,128)S(1)} copy(f32[8,5,16,136]{0,3,2,1:T(8,128)} %bitcast.1091) | data formatting | bytes 696320 | tf_op jit(solution)/shard_map/vmap()/add | solution.py:101
  143.5 6.2 %scatter.4 = f32[8,5,16,136]{3,0,2,1:T(8,128)S(1)} dynamic-update-slice(f32[8,5,16,136]{3,0,2,1:T(8,128)S(1)} %copy.542, f32[8,5,8,128]{3,0,2,1:T(8,128)S(1)} %copy-done.3, s32[]{:T(128)} %constant.88.clone.1, s32[]{:T(128)} %constant.88.clone.1, s32[]{:T(128)} %constant.182.clone.1, s32[]{:T(128)} %constant.182.clone.1) | dynamic-update-slice | bytes 327684 | tf_op jit(solution)/shard_map/scatter | solution.py:211
  160.4 3.5 %all-to-all-start.2 = ((f32[16,2,5,136]{3,1,2,0:T(2,128)}), f32[16,2,5,136]{3,1,2,0:T(2,128)S(1)}, u32[]{:S(2)}, u32[]{:S(2)}) async-start(f32[16,2,5,136]{3,1,2,0:T(2,128)} %copy.612), calls=%async_computation.2 | async-start | bytes 327680 | tf_op jit(solution)/shard_map/all_to_all | solution.py:222
  164.9 7.2 %all-to-all-done.2 = f32[16,2,5,136]{3,1,2,0:T(2,128)S(1)} async-done(((f32[16,2,5,136]{3,1,2,0:T(2,128)}), f32[16,2,5,136]{3,1,2,0:T(2,128)S(1)}, u32[]{:S(2)}, u32[]{:S(2)}) %all-to-all-start.2) | async-done | bytes 87072 | tf_op jit(solution)/shard_map/all_to_all | solution.py:222
  (353 shorter events, 62.0 us)
Async XLA Ops:
  0.6 7.8 %copy-start = (f32[8,5,8,128]{3,2,1,0:T(8,128)S(1)}, f32[8,5,8,128]{3,2,1,0:T(8,128)}, u32[]{:S(2)}) copy-start(f32[8,5,8,128]{3,2,1,0:T(8,128)} %param.7) | copy-start | bytes 491524
  0.6 5.2 %copy-start.1 = (s32[1024]{0:T(1024)S(1)}, s32[1024]{0:T(1024)}, u32[]{:S(2)}) copy-start(s32[1024]{0:T(1024)} %param.10) | copy-start | bytes 12292
  1.6 19.7 %collective-permute-start = (f32[5,3,512]{2,1,0:T(4,128)S(1)}, f32[5,3,512]{2,1,0:T(4,128)S(1)}, u32[]{:S(2)}, u32[]{:S(2)}) collective-permute-start(f32[5,3,512]{2,1,0:T(4,128)S(1)} %get-tuple-element.152), channel_id=1, source_target_pairs={{0,16},{16,32},{32,48},{48,64},{64,80},{80,96},{96,112},{112,0},{1... | collective-permute-start | bytes 92168 | tf_op jit(solution)/shard_map/ppermute | solution.py:24
  1.7 19.7 %collective-permute-start.1 = (f32[5,3,512]{2,1,0:T(4,128)S(1)}, f32[5,3,512]{2,1,0:T(4,128)S(1)}, u32[]{:S(2)}, u32[]{:S(2)}) collective-permute-start(f32[5,3,512]{2,1,0:T(4,128)S(1)} %get-tuple-element.153), channel_id=1, source_target_pairs={{16,0},{32,16},{48,32},{64,48},{80,64},{96,80},{112,96},{0,112},{1... | collective-permute-start | bytes 92168 | tf_op jit(solution)/shard_map/ppermute | solution.py:27
  5.9 15.5 %copy-start.2 = (f32[5,16,512]{2,1,0:T(8,128)S(1)}, f32[5,16,512]{2,1,0:T(8,128)}, u32[]{:S(2)}) copy-start(f32[5,16,512]{2,1,0:T(8,128)} %param.8) | copy-start | bytes 491524
  9.8 98.4 %all-to-all-start.1 = ((f32[16,1,5,8,128]{4,3,2,1,0:T(8,128)}), f32[16,1,5,8,128]{4,3,2,1,0:T(8,128)}, u32[]{:S(2)}, u32[]{:S(2)}) async-start(f32[16,1,5,8,128]{4,3,2,1,0:T(8,128)} %bitcast_select_fusion), calls=%async_computation.1 | async-start | bytes 655360 | tf_op jit(solution)/shard_map/all_to_all | solution.py:172
  19.8 74.3 %copy-start.18 = (pred[16,2]{0,1:T(4,128)(4,1)}, pred[16,2]{0,1:T(4,128)(4,1)S(1)}, u32[]{:S(2)}) copy-start(pred[16,2]{0,1:T(4,128)(4,1)S(1)} %fusion.103) | copy-start | bytes 100
  19.8 7.1 %copy-start.16 = (s32[16,2]{0,1:T(2,128)}, s32[16,2]{0,1:T(2,128)S(1)}, u32[]{:S(2)}) copy-start(s32[16,2]{0,1:T(2,128)S(1)} %select_reduce_fusion) | copy-start | bytes 388
  21.5 7.6 %collective-permute-start.2 = (f32[5,22,3]{2,1,0:T(8,128)S(1)}, f32[5,22,3]{2,1,0:T(8,128)S(1)}, u32[]{:S(2)}, u32[]{:S(2)}) collective-permute-start(f32[5,22,3]{2,1,0:T(8,128)S(1)} %get-tuple-element.148), channel_id=1, source_target_pairs={{0,1},{1,2},{2,3},{3,4},{4,5},{5,6},{6,7},{7,8},{8,9},{9,10},{10,1... | collective-permute-start | bytes 3968 | tf_op jit(solution)/shard_map/ppermute | solution.py:24
  23.4 5.7 %collective-permute-start.3 = (f32[5,22,3]{2,1,0:T(8,128)S(1)}, f32[5,22,3]{2,1,0:T(8,128)S(1)}, u32[]{:S(2)}, u32[]{:S(2)}) collective-permute-start(f32[5,22,3]{2,1,0:T(8,128)S(1)} %get-tuple-element.149), channel_id=1, source_target_pairs={{1,0},{2,1},{3,2},{4,3},{5,4},{6,5},{7,6},{8,7},{9,8},{10,9},{11,1... | collective-permute-start | bytes 3968 | tf_op jit(solution)/shard_map/ppermute | solution.py:27
  94.8 1.6 copy-start.7
  94.9 1.5 copy-start.9
  95.5 0.9 copy-start.11
  96.2 0.6 copy-start.12
  99.4 4.4 %copy-start.13 = (f32[5,16,2,1,64]{4,1,2,3,0:T(8,128)S(1)}, f32[5,16,2,1,64]{4,1,2,3,0:T(8,128)}, u32[]{:S(2)}) copy-start(f32[5,16,2,1,64]{4,1,2,3,0:T(8,128)} %copy-done.12) | copy-start | bytes 122884
  99.4 4.4 %copy-start.14 = (f32[1,16,2,64]{3,1,2,0:T(8,128)S(1)}, f32[1,16,2,64]{3,1,2,0:T(8,128)}, u32[]{:S(2)}) copy-start(f32[1,16,2,64]{3,1,2,0:T(8,128)} %get-tuple-element.59) | copy-start | bytes 24580
  101.2 16.2 %copy-start.22 = (pred[8]{0:T(512)(128)(4,1)S(1)}, pred[8]{0:T(512)(128)(4,1)}, u32[]{:S(2)}) copy-start(pred[8]{0:T(512)(128)(4,1)} %get-tuple-element.91) | copy-start | bytes 28
  101.9 4.8 %copy-start.8 = (f32[5,16,2,1,64]{4,1,2,3,0:T(8,128)S(1)}, f32[5,16,2,1,64]{4,1,2,3,0:T(8,128)}, u32[]{:S(2)}) copy-start(f32[5,16,2,1,64]{4,1,2,3,0:T(8,128)} %constant_dynamic-update-slice_fusion.40) | copy-start | bytes 122884
  102.5 12.6 %copy-start.10 = (f32[5,16,2,1,64]{4,1,2,3,0:T(8,128)S(1)}, f32[5,16,2,1,64]{4,1,2,3,0:T(8,128)}, u32[]{:S(2)}) copy-start(f32[5,16,2,1,64]{4,1,2,3,0:T(8,128)} %constant_dynamic-update-slice_fusion.50) | copy-start | bytes 122884
  108.2 18.7 %all-to-all-start = ((f32[16,2,5,10,70]{4,1,3,2,0:T(2,128)}), f32[16,2,5,10,70]{4,1,3,2,0:T(2,128)S(1)}, u32[]{:S(2)}, u32[]{:S(2)}) async-start(f32[16,2,5,10,70]{4,1,3,2,0:T(2,128)} %copy.529), calls=%async_computation | async-start | bytes 1638400 | tf_op jit(solution)/shard_map/all_to_all | solution.py:209
  128.8 2.8 %copy-start.20 = (f32[2]{0:T(128)S(1)}, f32[2]{0:T(128)}, u32[]{:S(2)}) copy-start(f32[2]{0:T(128)} %constant.196.clone) | copy-start | bytes 28
  138.9 4.6 %copy-start.3 = (f32[8,5,8,128]{3,0,2,1:T(8,128)S(1)}, f32[8,5,8,128]{3,0,2,1:T(8,128)}, u32[]{:S(2)}) copy-start(f32[8,5,8,128]{3,0,2,1:T(8,128)} %copy_select_fusion.2) | copy-start | bytes 491524
  157.9 1.0 copy-start.15
  157.9 1.6 copy-start.21
  158.1 14.0 %copy-start.4 = (f32[16,2,5,4]{3,0,2,1:T(8,128)S(1)}, f32[16,2,5,4]{3,0,2,1:T(8,128)}, u32[]{:S(2)}) copy-start(f32[16,2,5,4]{3,0,2,1:T(8,128)} %copy.596) | copy-start | bytes 7684
  158.1 14.0 %copy-start.5 = (f32[16,2,5,64]{3,0,2,1:T(8,128)S(1)}, f32[16,2,5,64]{3,0,2,1:T(8,128)}, u32[]{:S(2)}) copy-start(f32[16,2,5,64]{3,0,2,1:T(8,128)} %fusion.43) | copy-start | bytes 122884
  158.1 14.0 %copy-start.6 = (f32[16,2,5,64]{3,0,2,1:T(8,128)S(1)}, f32[16,2,5,64]{3,0,2,1:T(8,128)}, u32[]{:S(2)}) copy-start(f32[16,2,5,64]{3,0,2,1:T(8,128)} %fusion.44) | copy-start | bytes 122884
  158.1 14.0 %copy-start.17 = (s32[16,2]{0,1:T(2,128)S(1)}, s32[16,2]{0,1:T(2,128)}, u32[]{:S(2)}) copy-start(s32[16,2]{0,1:T(2,128)} %copy-done.16) | copy-start | bytes 388
  158.1 14.0 %copy-start.19 = (pred[16,2]{0,1:T(4,128)(4,1)S(1)}, pred[16,2]{0,1:T(4,128)(4,1)}, u32[]{:S(2)}) copy-start(pred[16,2]{0,1:T(4,128)(4,1)} %copy-done.18) | copy-start | bytes 100
  158.1 14.0 %copy-start.23 = (f32[136]{0:T(256)S(1)}, f32[136]{0:T(256)}, u32[]{:S(2)}) copy-start(f32[136]{0:T(256)} %constant.194.clone.1) | copy-start | bytes 1636
  160.4 11.7 %all-to-all-start.2 = ((f32[16,2,5,136]{3,1,2,0:T(2,128)}), f32[16,2,5,136]{3,1,2,0:T(2,128)S(1)}, u32[]{:S(2)}, u32[]{:S(2)}) async-start(f32[16,2,5,136]{3,1,2,0:T(2,128)} %copy.612), calls=%async_computation.2 | async-start | bytes 327680 | tf_op jit(solution)/shard_map/all_to_all | solution.py:222
where the time goes:
time: 174 us; the launch traced here: 173 us
  local copies, waits for them, and re-layouts  96.5 us (55%)
  other arithmetic  29.5 us (17%)
  starting transfers between devices  26.9 us (15%)
  waiting for transfers between devices  17.3 us (10%)
  between operations  1.84 us (1%)
    gather x96, local copies, waits for them, and re-layouts  63.8 us
    all_to_all x1, waiting for transfers between devices, local(): lax.all_to_all(blocks, 'gy', split_axis=0, concat_axis=0, tiled=True)  8.72 us
    all_to_all x1, starting transfers between devices, local(): lax.all_to_all(outgoing, 'gy', split_axis=0, concat_axis=0, tiled=True)  8.18 us
    all_to_all x1, waiting for transfers between devices, local(): lax.all_to_all(returning, 'gy', split_axis=0, concat_axis=0, tiled=True)  7.18 us
    all_to_all x1, starting transfers between devices, local(): lax.all_to_all(blocks, 'gy', split_axis=0, concat_axis=0, tiled=True)  6.84 us
    ppermute x2, starting transfers between devices, extended(): lax.ppermute(lax.slice_in_dim(block, 0, width, axis=dim), axis, backward)  6.41 us
    scatter x1, local copies, waits for them, and re-layouts, local(): padded = jax.vmap(prolong)(chosen).at[:, :, 4:-4, 4:-4].set(boxes_new)  6.21 us
    add x2, other arithmetic, prolong(): center[:, :, None, :, None]  4.89 us
  transfers between devices with their start and end apart: 7, of which 3 were waited for; matrix products, arithmetic and copies ran while one was open for 53% of the time, Pallas kernels for 0%

commit v1 on v0

v1 whole, which is shorter than its diff:
```python
import jax
import jax.numpy as jnp
from jax import lax
from jax.experimental import pallas as pl
from jax.experimental.pallas import tpu as pltpu
from jax.sharding import PartitionSpec as P

MESH = pl.DeviceIdType.MESH
F32 = jnp.float32
I32 = jnp.int32

GROUP = 16
SLABS = 8
GAMMA_LESS = 0.4
STEP_RATIO = 0.15
WAVE_SPEED = 2.5
HALF_STEP = 0.5 * STEP_RATIO
SUM_SCALE = 0.25 * STEP_RATIO * 0.5

T_DEV, T_LOC, T_OWN, T_RANK, T_BOX, T_POS, T_BACK, T_INV = 0, 1, 2, 3, 4, 5, 7, 9


def iota(axis):
    return lax.broadcasted_iota(I32, (8, 128), axis)


def shift_lanes(x, by):
    by = by % 128
    return x if by == 0 else pltpu.roll(x, by, axis=1)


def pick_lanes(x, index):
    return jnp.take_along_axis(x, index, axis=1)


def minmod(a, b):
    return jnp.maximum(jnp.minimum(a, b), 0.0) + jnp.minimum(jnp.maximum(a, b), 0.0)


def scaled_flux(state, along, sign):
    rho, m1, m2, m3, energy = state
    inverse = 1.0 / rho
    pressure = GAMMA_LESS * (energy - 0.5 * (m1 * m1 + m2 * m2 + m3 * m3) * inverse)
    normal = state[along] * inverse
    pieces = [state[along], m1 * normal, m2 * normal, m3 * normal, (energy + pressure) * normal]
    pieces[along] = pieces[along] + pressure
    speed = sign * WAVE_SPEED
    return [p + speed * u for p, u in zip(pieces, state)]


def cell_sides(low, mid, high, along):
    half = [0.5 * minmod(m - l, h - m) for l, m, h in zip(low, mid, high)]
    lower = scaled_flux([m - s for m, s in zip(mid, half)], along, -1.0)
    upper = scaled_flux([m + s for m, s in zip(mid, half)], along, 1.0)
    return lower, upper


def interface_flux(cells, along):
    a, b, c, d = cells
    left = [y + 0.5 * minmod(y - x, z - y) for x, y, z in zip(a, b, c)]
    right = [y - 0.5 * minmod(y - x, z - y) for x, y, z in zip(b, c, d)]
    upper = scaled_flux(left, along, 1.0)
    lower = scaled_flux(right, along, -1.0)
    return [u + l for u, l in zip(upper, lower)]


def make_tables(src_ref, pos_ref, gx, me, table):
    lane = iota(1)
    sub = iota(0)
    src = jnp.broadcast_to(src_ref[pl.ds(gx, 1), :], (8, 128)) & 127
    pos = jnp.broadcast_to(pos_ref[pl.ds(gx, 1), :], (8, 128)) & 511
    place = pick_lanes(pos, src)
    device = src >> 3
    local = src & 7
    owner = place >> 5
    spot = place & 31
    within = lane & 7
    group = lane >> 3
    rank = jnp.zeros((8, 128), I32)
    for d in range(1, 8):
        rank = rank + jnp.where((within >= d) & (shift_lanes(owner, d) == owner), 1, 0)

    def group_sum(v):
        for d in (1, 2, 4):
            v = v + shift_lanes(v, -d)
        return v

    mine = 8 * me + within
    my_owner = pick_lanes(owner, mine)
    my_rank = pick_lanes(rank, mine)
    rows = [device, local, owner, rank, group_sum(jnp.where(device == me, local, 0)) & 7]
    for a in range(2):
        rows.append(group_sum(jnp.where((owner == me) & (rank == a), spot, 0)) & 31)
    for a in range(2):
        rows.append(group_sum(jnp.where((my_owner == group) & (my_rank == a), within, 0)) & 7)
    inverse = jnp.zeros((8, 128), I32)
    for block in range(4):
        number = sub + 8 * block
        v = jnp.where((owner == me) & (spot == number), group * 2 + rank + 1, 0)
        for d in (64, 32, 16, 8, 4, 2, 1):
            v = v + shift_lanes(v, d)
        inverse = inverse + jnp.where(lane == number, v, 0)
    for d in (4, 2, 1):
        inverse = inverse + pltpu.roll(inverse, d, axis=0)
    rows.append(jnp.minimum(inverse, 32))
    for i, row in enumerate(rows):
        table[pl.ds(i, 1), :] = row[0:1, :]


def body(
    boxes, coarse, src_ref, pos_ref, fine_out, reflux_out,
    table, tabs, rim, strips, rows_x, cols_x, halo_send, halo_recv, edge_recv,
    box_send, box_recv, ghost_send, ghost_recv, sum_send, sum_recv,
    mixed, turned, coarse_c, coarse_s, state_a, state_b, low_y, high_y, faces_x, faces_y,
    back, fine_buf, sums_x, sums_y, line_x, line_y, own_x, own_y, out_x, out_y,
    table_sem, out_sem, halo_ss, halo_rs, box_ss, box_rs, ghost_ss, ghost_rs, sum_ss, sum_rs,
):
    gx = lax.axis_index("gx")
    me = lax.axis_index("gy")
    lane = iota(1)
    sub = iota(0)

    def peer(o):
        return lax.rem(me + o, GROUP)

    def slab(o):
        return lax.rem(gx + o + SLABS, SLABS)

    near = [(slab(1), me), (slab(-1), me)]
    corner = [(slab(dx), lax.rem(me + dy + GROUP, GROUP)) for dy in (-1, 1) for dx in (-1, 0, 1)]
    barrier = pltpu.get_barrier_semaphore()
    for o in range(1, GROUP):
        pl.semaphore_signal(barrier, inc=1, device_id=(gx, peer(o)), device_id_type=MESH)
    others = near + [corner[0], corner[2], corner[3], corner[5]]
    for there in others:
        pl.semaphore_signal(barrier, inc=1, device_id=there, device_id_type=MESH)

    make_tables(src_ref, pos_ref, gx, me, table)
    to_scalars = pltpu.make_async_copy(table, tabs, table_sem)
    to_scalars.start()

    for t in range(4):
        for f in range(5):
            tile = coarse[f, :, t * 128 : t * 128 + 128]
            halo_send[0, t, 3 * f : 3 * f + 3] = tile[13:16]
            halo_send[1, t, 3 * f : 3 * f + 3] = tile[0:3]
            rim[t * 5 + f, 8:24] = tile
            rim[20 + t * 5 + f, 8:24] = pltpu.roll(tile, 64, axis=1)
            rows_x[t, 22 * f + 3 : 22 * f + 19] = tile
    strips[0] = rows_x[0].T[0:8]
    strips[1] = rows_x[3].T[120:128]

    pl.semaphore_wait(barrier, GROUP - 1 + len(others))
    halo_copies = []
    for i, there in enumerate(near):
        halo_copies.append(
            pltpu.make_async_remote_copy(
                halo_send.at[i], halo_recv.at[i], halo_ss.at[i], halo_rs.at[i], there, MESH
            )
        )
    for i, there in enumerate(corner):
        halo_copies.append(
            pltpu.make_async_remote_copy(
                strips.at[i // 3], edge_recv.at[i], halo_ss.at[2 + i], halo_rs.at[2 + i], there, MESH
            )
        )
    for copy in halo_copies:
        copy.start()

    to_scalars.wait()

    def box_copy(o):
        return pltpu.make_async_remote_copy(
            box_send.at[o], box_recv.at[me], box_ss.at[o], box_rs.at[o], (gx, peer(o)), MESH
        )

    def ghost_copy(o):
        return pltpu.make_async_remote_copy(
            ghost_send.at[o], ghost_recv.at[me], ghost_ss.at[o], ghost_rs.at[o], (gx, peer(o)), MESH
        )

    def sum_copy(o):
        return pltpu.make_async_remote_copy(
            sum_send.at[o], sum_recv.at[me], sum_ss.at[o], sum_rs.at[o], (gx, peer(o)), MESH
        )

    def send_box(o, carry):
        which = tabs[T_BOX, 8 * peer(o)] & 7
        box_send[o] = boxes[which]
        box_copy(o).start()
        return carry

    lax.fori_loop(1, GROUP, send_box, 0)

    for copy in halo_copies:
        copy.wait_recv()
    for t in range(4):
        for f in range(5):
            top = halo_recv[0, t, 3 * f : 3 * f + 3]
            bottom = halo_recv[1, t, 3 * f : 3 * f + 3]
            rim[t * 5 + f, 5:8] = top
            rim[t * 5 + f, 24:27] = bottom
            rim[20 + t * 5 + f, 5:8] = pltpu.roll(top, 64, axis=1)
            rim[20 + t * 5 + f, 24:27] = pltpu.roll(bottom, 64, axis=1)
            rows_x[t, 22 * f : 22 * f + 3] = top
            rows_x[t, 22 * f + 19 : 22 * f + 22] = bottom
    for t in range(4):
        cols_x[8 + 128 * t : 136 + 128 * t] = rows_x[t].T
    field = jnp.zeros((8, 128), I32)
    for f in range(1, 5):
        field = field + jnp.where(lane >= 22 * f, 1, 0)
    place = lane - 22 * field
    for side, base in ((1, 0), (0, 520)):
        own = edge_recv[3 * side + 1]
        top = shift_lanes(edge_recv[3 * side + 2], -16)
        bottom = shift_lanes(edge_recv[3 * side], 16)
        cols_x[base : base + 8] = jnp.where(place < 3, top, jnp.where(place >= 19, bottom, own))

    first_lane = lane < 64
    top_rows = sub < 4
    tenth = jnp.zeros((8, 128), I32)
    for i in range(1, 12):
        tenth = tenth + jnp.where(lane >= 10 * i, 1, 0)
    side_index = jnp.where(lane < 100, 22 * jnp.where(tenth >= 5, tenth - 5, tenth) + lane - 10 * tenth, 0)

    def pack_ghosts(o, dest, slot):
        at = 8 * peer(o)
        spots = [tabs[T_POS, at] & 31, tabs[T_POS + 1, at] & 31]
        rs = [s >> 3 for s in spots]
        cs = [s & 7 for s in spots]
        ids = [(((c & 1) ^ a) * 4 + (c >> 1)) * 5 for a, c in enumerate(cs)]
        for f in range(5):
            parts = [
                jnp.where(
                    top_rows, rim[ids[a] + f, pl.ds(4 * rs[a] + 5, 8), :], rim[ids[a] + f, pl.ds(4 * rs[a] + 7, 8), :]
                )
                for a in range(2)
            ]
            dest[slot, f] = jnp.where(first_lane, parts[0], parts[1])
        sides = []
        for a in range(2):
            strip = jnp.where(
                top_rows, cols_x[pl.ds(64 * cs[a] + 5, 8), :], cols_x[pl.ds(64 * cs[a] + 67, 8), :]
            )
            sides.append(pick_lanes(strip, side_index + 4 * rs[a]))
        dest[slot, 5] = jnp.where(lane < 50, sides[0], sides[1])

    def send_ghosts(o, carry):
        pack_ghosts(o, ghost_send, o)
        ghost_copy(o).start()
        return carry

    lax.fori_loop(1, GROUP, send_ghosts, 0)
    pack_ghosts(0, ghost_recv, me)

    scale_x = jnp.where(first_lane, HALF_STEP, -HALF_STEP)
    for t in range(4):
        cells = [
            [rim[t * 5 + f, pl.ds(8 + k, 8, stride=4), :] for f in range(5)] for k in (-2, -1, 0, 1)
        ]
        flux = interface_flux(cells, 1)
        for f in range(5):
            line_x[t, pl.ds(f, 8, stride=8), :] = flux[f]
    for f5 in range(2):
        cells = [
            [
                shift_lanes(cols_x[pl.ds(8 + k + 512 * f5, 8, stride=64), :], -(22 * f + 3))
                for f in range(5)
            ]
            for k in (-2, -1, 0, 1)
        ]
        flux = interface_flux(cells, 2)
        for f in range(5):
            line_y[pl.ds(64 * f5 + f, 8, stride=8), :] = flux[f]
    scale_y = jnp.where(lane < 4, HALF_STEP, -HALF_STEP)
    for r in range(4):
        for t in range(4):
            low = line_x[t, 8 * r : 8 * r + 8]
            high = line_x[t, 8 * r + 8 : 8 * r + 16]
            own_x[8 * r + 2 * t] = scale_x * jnp.where(first_lane, low, shift_lanes(high, 64))
            own_x[8 * r + 2 * t + 1] = scale_x * jnp.where(first_lane, shift_lanes(low, 64), high)
        for c in range(8):
            low = line_y[8 * c : 8 * c + 8]
            high = line_y[8 * c + 8 : 8 * c + 16]
            own_y[8 * r + c] = scale_y * jnp.where(
                lane < 4, shift_lanes(low, -4 * r), shift_lanes(high, 4 - 4 * r)
            )

    def wait_boxes(o, carry):
        box_copy(o).wait_recv()
        return carry

    def wait_ghosts(o, carry):
        ghost_copy(o).wait_recv()
        return carry

    lax.fori_loop(1, GROUP, wait_boxes, 0)
    lax.fori_loop(1, GROUP, wait_ghosts, 0)
    side_parts = [jnp.zeros((8, 128), F32) for _ in range(5)]
    for b in range(8):
        at = 8 * me + b
        device = tabs[T_DEV, at] & 15
        local = tabs[T_LOC, at] & 7
        owner = tabs[T_OWN, at] & 15
        second = tabs[T_RANK, at] == 1
        stays = device == me
        for f in range(5):
            box = jnp.where(stays, boxes[local, f], box_recv[device, f])
            inner = ghost_recv[owner, f]
            inner = jnp.where(second, shift_lanes(inner, 64), inner)
            mixed[f, 16 * b : 16 * b + 8] = inner
            mixed[f, 16 * b + 8 : 16 * b + 16] = box
        side = ghost_recv[owner, 5]
        side = jnp.where(second, shift_lanes(side, -50), side)
        for f in range(5):
            side_parts[f] = jnp.where((lane >> 4) == b, shift_lanes(side, 16 * b - 10 * f), side_parts[f])

    ring = (lane - 4) & 127
    row = ring & 15
    base = ring - row
    coarse_row = (row >> 1) + 1

    def kept(i):
        return jnp.where(i < 4, i, jnp.where(i < 6, 3, i - 2))

    inner_index = [base + kept(coarse_row + d) for d in (0, -1, 1)]
    side_rows = [base + coarse_row + d for d in (0, -1, 1)]
    interior = (lane & 8) != 0
    row_sign = jnp.where((row & 1) == 0, -0.25, 0.25)
    for f in range(5):
        turned[f] = mixed[f].T
        for k in range(8):
            block = turned[f, 8 * k : 8 * k + 8]
            mid, low, high = [pick_lanes(block, index) for index in inner_index]
            coarse_c[f, 3 + 8 * k : 11 + 8 * k] = mid
            coarse_s[f, 3 + 8 * k : 11 + 8 * k] = row_sign * minmod(mid - low, high - mid)
        mid, low, high = [pick_lanes(side_parts[f], index) for index in side_rows]
        slope = row_sign * minmod(mid - low, high - mid)
        coarse_c[f, 0:4] = mid[0:4]
        coarse_c[f, 66:70] = mid[4:8]
        coarse_s[f, 0:4] = slope[0:4]
        coarse_s[f, 66:70] = slope[4:8]
        for k in range(9):
            j = 1 + 8 * k
            mid = coarse_c[f, j : j + 8]
            slope = minmod(mid - coarse_c[f, j - 1 : j + 7], coarse_c[f, j + 1 : j + 9] - mid)
            middle = mid + coarse_s[f, j : j + 8]
            state_a[f, pl.ds(2 * j - 2, 8, stride=2), :] = middle - 0.25 * slope
            state_a[f, pl.ds(2 * j - 1, 8, stride=2), :] = middle + 0.25 * slope
        for k in range(16):
            m = 4 + 8 * k
            state_a[f, m : m + 8] = jnp.where(interior, turned[f, 8 * k : 8 * k + 8], state_a[f, m : m + 8])

    lower_face = (lane & 15) == 7

    def step(state, result, last):
        def chunk(k, carry):
            m = pl.multiple_of(8 * k, 8)
            mid = [state[f, pl.ds(m + 1, 8), :] for f in range(5)]
            low = [state[f, pl.ds(m, 8), :] for f in range(5)]
            high = [state[f, pl.ds(m + 2, 8), :] for f in range(5)]
            lower, upper = cell_sides(low, mid, high, 2)
            for f in range(5):
                low_y[f, pl.ds(m + 9, 8), :] = lower[f]
                high_y[f, pl.ds(m + 9, 8), :] = upper[f]
            cells = low
            lower, upper = cell_sides(
                [shift_lanes(u, 1) for u in cells], cells, [shift_lanes(u, -1) for u in cells], 1
            )
            for f in range(5):
                after = upper[f] + shift_lanes(lower[f], -1)
                before = shift_lanes(upper[f], 1) + lower[f]
                after_y = high_y[f, pl.ds(m + 8, 8), :] + low_y[f, pl.ds(m + 9, 8), :]
                before_y = high_y[f, pl.ds(m + 7, 8), :] + low_y[f, pl.ds(m + 8, 8), :]
                new = cells[f] - HALF_STEP * (after - before) - HALF_STEP * (after_y - before_y)
                face = jnp.where(lower_face, after, before)
                if last:
                    face = face + faces_x[f, pl.ds(m, 8), :]
                    result[f, pl.ds(m, 8), :] = jnp.where(interior, new, face)
                else:
                    faces_x[f, pl.ds(m, 8), :] = face
                    result[f, pl.ds(m, 8), :] = new
            return carry

        lax.fori_loop(0, 17, chunk, 0)
        for f in range(5):
            for i, m in enumerate((3, 131)):
                flux = high_y[f, m + 8 : m + 9] + low_y[f, m + 9 : m + 10]
                if last:
                    flux = flux + faces_y[i, f : f + 1]
                faces_y[i, f : f + 1] = flux

    step(state_a, state_b, False)
    step(state_b, state_a, True)

    pair_index = 2 * (lane & 63)
    for f in range(5):
        back[f, 0:128] = state_a[f, 4:132].T
        back[f, 128:136] = back[f, 0:8]
        for b in range(8):
            fine_buf[b, f] = back[f, 16 * b + 8 : 16 * b + 16]
        low = back[f, pl.ds(7, 8, stride=16), :]
        high = back[f, pl.ds(16, 8, stride=16), :]
        low = low + shift_lanes(low, -1)
        high = high + shift_lanes(high, -1)
        sums_x[pl.ds(f, 8, stride=8), :] = jnp.where(
            first_lane, pick_lanes(low, pair_index), pick_lanes(high, pair_index)
        )
    to_fine = pltpu.make_async_copy(fine_buf, fine_out, out_sem)
    low = faces_y[0] + shift_lanes(faces_y[0], -1)
    high = faces_y[1] + shift_lanes(faces_y[1], -1)
    for b in range(8):
        index = 16 * b + 8 + 2 * (lane & 3)
        sums_y[b] = jnp.where((lane & 4) == 0, pick_lanes(low, index), pick_lanes(high, index))

    def pack_sums(o, dest, slot):
        at = 8 * peer(o)
        first = tabs[T_BACK, at] & 7
        second = tabs[T_BACK + 1, at] & 7
        dest[slot, 0:8] = sums_x[pl.ds(8 * first, 8), :]
        dest[slot, 5:13] = sums_x[pl.ds(8 * second, 8), :]
        dest[slot, 10:16] = jnp.where(lane < 8, sums_y[first], sums_y[second])[0:6]

    def send_sums(o, carry):
        pack_sums(o, sum_send, o)
        sum_copy(o).start()
        return carry

    def wait_sums(o, carry):
        sum_copy(o).wait_recv()
        return carry

    lax.fori_loop(1, GROUP, send_sums, 0)
    pack_sums(0, sum_recv, me)
    to_fine.start()

    for copy in halo_copies:
        copy.wait_send()

    def wait_sent(o, carry):
        box_copy(o).wait_send()
        ghost_copy(o).wait_send()
        return carry

    lax.fori_loop(1, GROUP, wait_sent, 0)
    lax.fori_loop(1, GROUP, wait_sums, 0)

    sign_x = jnp.where(first_lane, SUM_SCALE, -SUM_SCALE)
    for n in range(32):
        entry = tabs[T_INV, n]
        live = entry > 0
        slot = (entry - 1) & 31
        sender = slot >> 1
        second = (slot & 1) == 1
        total_x = sum_recv[sender, pl.ds(5 * (slot & 1), 8), :]
        total_y = sum_recv[sender, pl.ds(10, 6), :]
        total_y = jnp.where(second, pltpu.roll(total_y, 120, axis=1), total_y)
        sign_y = jnp.where(lane[0:5] < 4, SUM_SCALE, -SUM_SCALE)
        out_x[pl.ds(n, 5, stride=32), :] = jnp.where(live, own_x[n, 0:5] - sign_x[0:5] * total_x[0:5], 0.0)
        out_y[pl.ds(n, 5, stride=32), :] = jnp.where(live, own_y[n, 0:5] - sign_y * total_y[0:5], 0.0)
    for f in range(5):
        reflux_out[f, :, 0:128] = out_x[32 * f : 32 * f + 32]
        reflux_out[f, :, 128:136] = out_y[32 * f : 32 * f + 32][:, 0:8]

    def wait_sums_sent(o, carry):
        sum_copy(o).wait_send()
        return carry

    lax.fori_loop(1, GROUP, wait_sums_sent, 0)
    to_fine.wait()


def local(previous_fine_boxes, coarse_state, new_source, box_position):
    vmem = pl.BlockSpec(memory_space=pltpu.VMEM)
    dma = pltpu.SemaphoreType.DMA
    v = pltpu.VMEM
    fine, reflux = pl.pallas_call(
        body,
        out_shape=(
            jax.ShapeDtypeStruct((8, 5, 8, 128), F32),
            jax.ShapeDtypeStruct((5, 32, 136), F32),
        ),
        in_specs=[vmem] * 4,
        out_specs=(pl.BlockSpec(memory_space=pl.ANY), vmem),
        scratch_shapes=[
            v((16, 128), I32),
            pltpu.SMEM((16, 128), I32),
            v((40, 48, 128), F32),
            v((2, 8, 128), F32),
            v((4, 128, 128), F32),
            v((1040, 128), F32),
            v((2, 4, 16, 128), F32),
            v((2, 4, 16, 128), F32),
            v((6, 8, 128), F32),
            v((16, 5, 8, 128), F32),
            v((16, 5, 8, 128), F32),
            v((16, 6, 8, 128), F32),
            v((16, 6, 8, 128), F32),
            v((16, 16, 128), F32),
            v((16, 16, 128), F32),
            v((5, 128, 128), F32),
            v((5, 128, 128), F32),
            v((5, 80, 128), F32),
            v((5, 80, 128), F32),
            v((5, 152, 128), F32),
            v((5, 152, 128), F32),
            v((5, 160, 128), F32),
            v((5, 160, 128), F32),
            v((5, 136, 128), F32),
            v((2, 8, 128), F32),
            v((5, 144, 128), F32),
            v((8, 5, 8, 128), F32),
            v((72, 128), F32),
            v((8, 8, 128), F32),
            v((4, 72, 128), F32),
            v((136, 128), F32),
            v((32, 8, 128), F32),
            v((32, 8, 128), F32),
            v((192, 128), F32),
            v((192, 128), F32),
            dma,
            dma,
            dma((8,)),
            dma((8,)),
            dma((16,)),
            dma((16,)),
            dma((16,)),
            dma((16,)),
            dma((16,)),
            dma((16,)),
        ],
        compiler_params=pltpu.CompilerParams(
            collective_id=0, has_side_effects=True, vmem_limit_bytes=40 * 1024 * 1024
        ),
    )(
        previous_fine_boxes,
        coarse_state,
        new_source.reshape(8, 128),
        box_position.reshape(8, 128),
    )
    return fine, jnp.transpose(reflux, (1, 0, 2))


def solution(mesh):
    placed = (P(("gx", "gy"), None, None, None), P(None, "gx", "gy"), P(), P())
    return jax.shard_map(
        local,
        mesh=mesh,
        in_specs=placed,
        out_specs=(P(("gx", "gy"), None, None, None), P(("gx", "gy"), None, None)),
        check_vma=False,
    )
```

time: 174 us -> 38.4 us (0.22)
  local copies, waits for them, and re-layouts: 96.5 us -> 4.53 us
  Pallas kernels: 0 us -> 33 us
  other arithmetic: 29.5 us -> 0 us
  starting transfers between devices: 26.9 us -> 0 us
  waiting for transfers between devices: 17.3 us -> 0 us
    gather x104 -> x0, local copies, waits for them, and re-layouts: 69 us -> none
    pallas_call x0 -> x1, Pallas kernels: none -> 33 us  [local(): pl.pallas_call(body, out_shape=(jax.ShapeDtypeStruct((8, 5, 8, 128), F32)...]
    all_to_all x3 -> x0, starting transfers between devices: 18.5 us -> none  [the longest x1 8.18 us: local(): lax.all_to_all(outgoing, 'gy', split_axis=0, concat_axis=0, tiled=True)]
    all_to_all x3 -> x0, waiting for transfers between devices: 15.9 us -> none  [the longest x1 8.72 us: local(): lax.all_to_all(blocks, 'gy', split_axis=0, concat_axis=0, tiled=True)]
    ppermute x4 -> x0, starting transfers between devices: 8.37 us -> none  [the longest x2 6.41 us: extended(): lax.ppermute(lax.slice_in_dim(block, 0, width, axis=dim), axis, backward)]
    scatter x1 -> x0, local copies, waits for them, and re-layouts: 6.21 us -> none  [local(): padded = jax.vmap(prolong)(chosen).at[:, :, 4:-4, 4:-4].set(boxes_new)]
    add x9 -> x0, other arithmetic: 6.21 us -> none  [the longest x2 4.89 us: prolong(): center[:, :, None, :, None]]
    slice x26 -> x0, local copies, waits for them, and re-layouts: 4.69 us -> none  [the longest x1 0.99 us: extended(): lax.slice_in_dim(block, block.shape[dim] - width, None, axis=dim)]
  transfers between devices with their start and end apart: 7 -> 0, of which waited for: 3 -> 0; matrix products, arithmetic and copies ran while one was open for 53% -> 0% of each run, Pallas kernels for 0% -> 0%
where the time goes in v1:
time: 38.4 us; the launch traced here: 38.2 us
  Pallas kernels  33 us (86%)
  local copies, waits for them, and re-layouts  4.53 us (12%)
  between operations  0.65 us (2%)
    pallas_call x1, Pallas kernels, local(): pl.pallas_call(body, out_shape=(jax.ShapeDtypeStruct((8, 5, 8, 128), F32)...  33 us
    unnamed x10, local copies, waits for them, and re-layouts  4.53 us

profile of v1, /device:TPU:0, one launch (start us, length us, event | category | flops | bytes accessed | tf_op | source)
XLA Modules:
  0.0 38.2 jit_solution(15693290327992784347)
XLA Ops:
  0.6 0.0 copy-start
  0.6 0.9 %copy-done = f32[8,5,8,128]{3,2,1,0:T(8,128)S(1)} copy-done((f32[8,5,8,128]{3,2,1,0:T(8,128)S(1)}, f32[8,5,8,128]{3,2,1,0:T(8,128)}, u32[]{:S(2)}) %copy-start) | copy-done | bytes 163864
  1.5 0.0 copy-start.1
  1.5 0.9 %copy-done.1 = f32[5,16,512]{2,1,0:T(8,128)S(1)} copy-done((f32[5,16,512]{2,1,0:T(8,128)S(1)}, f32[5,16,512]{2,1,0:T(8,128)}, u32[]{:S(2)}) %copy-start.1) | copy-done | bytes 163864
  2.5 0.0 copy-start.2
  2.5 0.7 %copy-done.2 = s32[1024]{0:T(1024)S(1)} copy-done((s32[1024]{0:T(1024)S(1)}, s32[1024]{0:T(1024)}, u32[]{:S(2)}) %copy-start.2) | copy-done | bytes 4120
  3.2 0.0 copy-start.3
  3.2 0.7 %copy-done.3 = s32[1024]{0:T(1024)S(1)} copy-done((s32[1024]{0:T(1024)S(1)}, s32[1024]{0:T(1024)}, u32[]{:S(2)}) %copy-start.3) | copy-done | bytes 4120
  3.8 33.0 %shard_map.59 = (f32[8,5,8,128]{3,2,1,0:T(8,128)S(1)}, f32[5,32,136]{2,1,0:T(8,128)S(1)}) custom-call(f32[8,5,8,128]{3,2,1,0:T(8,128)S(1)} %copy-done, f32[5,16,512]{2,1,0:T(8,128)S(1)} %copy-done.1, s32[8,128]{1,0:T(8,128)S(1)} %bitcast.4, s32[8,128]{1,0:T(8,128)S(1)} %bitcast.5), custom_call_target="tpu_custom_call" | custom-call | tf_op jit(solution)/shard_map/pallas_call | solution.py:477
  36.9 0.7 %copy.8 = f32[8,5,8,128]{3,2,1,0:T(8,128)} copy(f32[8,5,8,128]{3,2,1,0:T(8,128)S(1)} %get-tuple-element.8) | data formatting | bytes 327680
  37.5 0.7 %copy.9 = f32[32,5,136]{2,0,1:T(8,128)} copy(f32[32,5,136]{2,0,1:T(8,128)S(1)} %bitcast.3) | data formatting | bytes 174080
Async XLA Ops:
  0.6 0.9 %copy-start = (f32[8,5,8,128]{3,2,1,0:T(8,128)S(1)}, f32[8,5,8,128]{3,2,1,0:T(8,128)}, u32[]{:S(2)}) copy-start(f32[8,5,8,128]{3,2,1,0:T(8,128)} %boxes.1) | copy-start | bytes 491524
  1.5 0.9 %copy-start.1 = (f32[5,16,512]{2,1,0:T(8,128)S(1)}, f32[5,16,512]{2,1,0:T(8,128)}, u32[]{:S(2)}) copy-start(f32[5,16,512]{2,1,0:T(8,128)} %coarse.1) | copy-start | bytes 491524
  2.5 0.7 %copy-start.2 = (s32[1024]{0:T(1024)S(1)}, s32[1024]{0:T(1024)}, u32[]{:S(2)}) copy-start(s32[1024]{0:T(1024)} %param.6) | copy-start | bytes 12292
  3.2 0.7 %copy-start.3 = (s32[1024]{0:T(1024)S(1)}, s32[1024]{0:T(1024)}, u32[]{:S(2)}) copy-start(s32[1024]{0:T(1024)} %param.7) | copy-start | bytes 12292

commit v2 on v1

--- a/solution.py
+++ b/solution.py
@@ -17,7 +17,8 @@
 HALF_STEP = 0.5 * STEP_RATIO
 SUM_SCALE = 0.25 * STEP_RATIO * 0.5
 
-T_DEV, T_LOC, T_OWN, T_RANK, T_BOX, T_POS, T_BACK, T_INV = 0, 1, 2, 3, 4, 5, 7, 9
+T_DEV, T_LOC, T_OWN, T_RANK, T_SPOT, T_BOX, T_INV = 0, 1, 2, 3, 4, 5, 6
+T_POS, T_POS_NEXT, T_POS_BEFORE, T_BACK = 8, 10, 12, 14
 
 
 def iota(axis):
@@ -34,18 +35,21 @@
 
 
 def minmod(a, b):
-    return jnp.maximum(jnp.minimum(a, b), 0.0) + jnp.minimum(jnp.maximum(a, b), 0.0)
+    return jnp.maximum(jnp.minimum(a, b), jnp.minimum(jnp.maximum(a, b), 0.0))
 
 
 def scaled_flux(state, along, sign):
     rho, m1, m2, m3, energy = state
+    speed = sign * WAVE_SPEED
     inverse = 1.0 / rho
     pressure = GAMMA_LESS * (energy - 0.5 * (m1 * m1 + m2 * m2 + m3 * m3) * inverse)
     normal = state[along] * inverse
-    pieces = [state[along], m1 * normal, m2 * normal, m3 * normal, (energy + pressure) * normal]
+    moved = normal + speed
+    pieces = [
+        state[along] + speed * rho, m1 * moved, m2 * moved, m3 * moved, energy * moved + pressure * normal
+    ]
     pieces[along] = pieces[along] + pressure
-    speed = sign * WAVE_SPEED
-    return [p + speed * u for p, u in zip(pieces, state)]
+    return pieces
 
 
 def cell_sides(low, mid, high, along):
@@ -88,11 +92,9 @@
     mine = 8 * me + within
     my_owner = pick_lanes(owner, mine)
     my_rank = pick_lanes(rank, mine)
-    rows = [device, local, owner, rank, group_sum(jnp.where(device == me, local, 0)) & 7]
-    for a in range(2):
-        rows.append(group_sum(jnp.where((owner == me) & (rank == a), spot, 0)) & 31)
-    for a in range(2):
-        rows.append(group_sum(jnp.where((my_owner == group) & (my_rank == a), within, 0)) & 7)
+    after = (me + 1) & 15
+    before = (me + 15) & 15
+    rows = [device, local, owner, rank, spot, group_sum(jnp.where(device == me, local, 0)) & 7]
     inverse = jnp.zeros((8, 128), I32)
     for block in range(4):
         number = sub + 8 * block
@@ -102,18 +104,23 @@
         inverse = inverse + jnp.where(lane == number, v, 0)
     for d in (4, 2, 1):
         inverse = inverse + pltpu.roll(inverse, d, axis=0)
-    rows.append(jnp.minimum(inverse, 32))
+    rows += [jnp.minimum(inverse, 32), rank]
+    for whose in (me, after, before):
+        for a in range(2):
+            rows.append(group_sum(jnp.where((owner == whose) & (rank == a), spot, 0)) & 31)
+    for a in range(2):
+        rows.append(group_sum(jnp.where((my_owner == group) & (my_rank == a), within, 0)) & 7)
     for i, row in enumerate(rows):
         table[pl.ds(i, 1), :] = row[0:1, :]
 
 
 def body(
-    boxes, coarse, src_ref, pos_ref, fine_out, reflux_out,
-    table, tabs, rim, strips, rows_x, cols_x, halo_send, halo_recv, edge_recv,
+    boxes_in, coarse_in, src_in, pos_in, fine_out, reflux_out,
+    boxes, coarse, src_ref, pos_ref, table, tabs, rim, rows_x, cols_x, halo_send, halo_recv, edge_recv,
     box_send, box_recv, ghost_send, ghost_recv, sum_send, sum_recv,
-    mixed, turned, coarse_c, coarse_s, state_a, state_b, low_y, high_y, faces_x, faces_y,
-    back, fine_buf, sums_x, sums_y, line_x, line_y, own_x, own_y, out_x, out_y,
-    table_sem, out_sem, halo_ss, halo_rs, box_ss, box_rs, ghost_ss, ghost_rs, sum_ss, sum_rs,
+    mixed, turned, coarse_c, coarse_s, state_a, state_b, low_y, high_y, low_x, high_x, change_x, faces_x, faces_y,
+    face_cols, face_rows, back, sums_x, sums_y, line_x, line_y, own_x, own_y, out_x, out_y,
+    table_sem, in_sem, halo_ss, halo_rs, box_ss, box_rs, ghost_ss, ghost_rs, sum_ss, sum_rs,
 ):
     gx = lax.axis_index("gx")
     me = lax.axis_index("gy")
@@ -127,18 +134,28 @@
         return lax.rem(gx + o + SLABS, SLABS)
 
     near = [(slab(1), me), (slab(-1), me)]
-    corner = [(slab(dx), lax.rem(me + dy + GROUP, GROUP)) for dy in (-1, 1) for dx in (-1, 0, 1)]
+    beside = [(gx, peer(GROUP - 1)), (gx, peer(1))]
     barrier = pltpu.get_barrier_semaphore()
-    for o in range(1, GROUP):
+    for there in near:
+        pl.semaphore_signal(barrier, inc=1, device_id=there, device_id_type=MESH)
+    for o in (1, 15, 4, 12, 2, 14, 8, 3, 13, 5, 11, 6, 10, 7, 9):
         pl.semaphore_signal(barrier, inc=1, device_id=(gx, peer(o)), device_id_type=MESH)
-    others = near + [corner[0], corner[2], corner[3], corner[5]]
-    for there in others:
-        pl.semaphore_signal(barrier, inc=1, device_id=there, device_id_type=MESH)
-
+    fetches = [
+        pltpu.make_async_copy(coarse_in, coarse, in_sem.at[0]),
+        pltpu.make_async_copy(src_in, src_ref, in_sem.at[1]),
+        pltpu.make_async_copy(pos_in, pos_ref, in_sem.at[2]),
+        pltpu.make_async_copy(boxes_in, boxes, in_sem.at[3]),
+    ]
+    for fetch in fetches:
+        fetch.start()
+
+    fetches[1].wait()
+    fetches[2].wait()
     make_tables(src_ref, pos_ref, gx, me, table)
     to_scalars = pltpu.make_async_copy(table, tabs, table_sem)
     to_scalars.start()
 
+    fetches[0].wait()
     for t in range(4):
         for f in range(5):
             tile = coarse[f, :, t * 128 : t * 128 + 128]
@@ -147,10 +164,8 @@
             rim[t * 5 + f, 8:24] = tile
             rim[20 + t * 5 + f, 8:24] = pltpu.roll(tile, 64, axis=1)
             rows_x[t, 22 * f + 3 : 22 * f + 19] = tile
-    strips[0] = rows_x[0].T[0:8]
-    strips[1] = rows_x[3].T[120:128]
-
-    pl.semaphore_wait(barrier, GROUP - 1 + len(others))
+
+    pl.semaphore_wait(barrier, GROUP + 1)
     halo_copies = []
     for i, there in enumerate(near):
         halo_copies.append(
@@ -158,16 +173,11 @@
                 halo_send.at[i], halo_recv.at[i], halo_ss.at[i], halo_rs.at[i], there, MESH
             )
         )
-    for i, there in enumerate(corner):
-        halo_copies.append(
-            pltpu.make_async_remote_copy(
-                strips.at[i // 3], edge_recv.at[i], halo_ss.at[2 + i], halo_rs.at[2 + i], there, MESH
-            )
-        )
     for copy in halo_copies:
         copy.start()
 
     to_scalars.wait()
+    fetches[3].wait()
 
     def box_copy(o):
         return pltpu.make_async_remote_copy(
@@ -206,15 +216,14 @@
             rows_x[t, 22 * f + 19 : 22 * f + 22] = bottom
     for t in range(4):
         cols_x[8 + 128 * t : 136 + 128 * t] = rows_x[t].T
-    field = jnp.zeros((8, 128), I32)
-    for f in range(1, 5):
-        field = field + jnp.where(lane >= 22 * f, 1, 0)
-    place = lane - 22 * field
-    for side, base in ((1, 0), (0, 520)):
-        own = edge_recv[3 * side + 1]
-        top = shift_lanes(edge_recv[3 * side + 2], -16)
-        bottom = shift_lanes(edge_recv[3 * side], 16)
-        cols_x[base : base + 8] = jnp.where(place < 3, top, jnp.where(place >= 19, bottom, own))
+    edge_copies = [
+        pltpu.make_async_remote_copy(
+            cols_x.at[pl.ds(at, 8)], edge_recv.at[i], halo_ss.at[2 + i], halo_rs.at[2 + i], there, MESH
+        )
+        for i, (at, there) in enumerate(zip((8, 512), beside))
+    ]
+    for copy in edge_copies:
+        copy.start()
 
     first_lane = lane < 64
     top_rows = sub < 4
@@ -244,6 +253,13 @@
             )
             sides.append(pick_lanes(strip, side_index + 4 * rs[a]))
         dest[slot, 5] = jnp.where(lane < 50, sides[0], sides[1])
+        edge = jnp.where(top_rows, cols_x[517:525], cols_x[3:11])
+        edges = []
+        for a in range(2):
+            low = (tabs[T_POS_NEXT + a, at] & 31) >> 3
+            high = (tabs[T_POS_BEFORE + a, at] & 31) >> 3
+            edges.append(pick_lanes(edge, side_index + 4 * jnp.where(top_rows, low, high)))
+        dest[slot, 6] = jnp.where(lane < 50, edges[0], edges[1])
 
     def send_ghosts(o, carry):
         pack_ghosts(o, ghost_send, o)
@@ -261,6 +277,10 @@
         flux = interface_flux(cells, 1)
         for f in range(5):
             line_x[t, pl.ds(f, 8, stride=8), :] = flux[f]
+    for copy in edge_copies:
+        copy.wait_recv()
+    cols_x[0:8] = edge_recv[1]
+    cols_x[520:528] = edge_recv[0]
     for f5 in range(2):
         cells = [
             [
@@ -310,7 +330,12 @@
             inner = jnp.where(second, shift_lanes(inner, 64), inner)
             mixed[f, 16 * b : 16 * b + 8] = inner
             mixed[f, 16 * b + 8 : 16 * b + 16] = box
+        column = tabs[T_SPOT, at] & 7
+        low_edge = ghost_recv[(owner + 15) & 15, 6]
+        high_edge = ghost_recv[(owner + 1) & 15, 6]
         side = ghost_recv[owner, 5]
+        side = jnp.where((sub < 3) & (column == 0), low_edge, side)
+        side = jnp.where((sub >= 5) & (column == 7), high_edge, side)
         side = jnp.where(second, shift_lanes(side, -50), side)
         for f in range(5):
             side_parts[f] = jnp.where((lane >> 4) == b, shift_lanes(side, 16 * b - 10 * f), side_parts[f])
@@ -353,60 +378,82 @@
 
     lower_face = (lane & 15) == 7
 
-    def step(state, result, last):
-        def chunk(k, carry):
-            m = pl.multiple_of(8 * k, 8)
-            mid = [state[f, pl.ds(m + 1, 8), :] for f in range(5)]
-            low = [state[f, pl.ds(m, 8), :] for f in range(5)]
-            high = [state[f, pl.ds(m + 2, 8), :] for f in range(5)]
-            lower, upper = cell_sides(low, mid, high, 2)
-            for f in range(5):
-                low_y[f, pl.ds(m + 9, 8), :] = lower[f]
-                high_y[f, pl.ds(m + 9, 8), :] = upper[f]
-            cells = low
-            lower, upper = cell_sides(
-                [shift_lanes(u, 1) for u in cells], cells, [shift_lanes(u, -1) for u in cells], 1
-            )
-            for f in range(5):
-                after = upper[f] + shift_lanes(lower[f], -1)
-                before = shift_lanes(upper[f], 1) + lower[f]
-                after_y = high_y[f, pl.ds(m + 8, 8), :] + low_y[f, pl.ds(m + 9, 8), :]
-                before_y = high_y[f, pl.ds(m + 7, 8), :] + low_y[f, pl.ds(m + 8, 8), :]
-                new = cells[f] - HALF_STEP * (after - before) - HALF_STEP * (after_y - before_y)
-                face = jnp.where(lower_face, after, before)
-                if last:
-                    face = face + faces_x[f, pl.ds(m, 8), :]
-                    result[f, pl.ds(m, 8), :] = jnp.where(interior, new, face)
-                else:
-                    faces_x[f, pl.ds(m, 8), :] = face
-                    result[f, pl.ds(m, 8), :] = new
-            return carry
-
-        lax.fori_loop(0, 17, chunk, 0)
+    def y_sides(state, m):
+        lower, upper = cell_sides(
+            [state[f, m : m + 8] for f in range(5)],
+            [state[f, m + 1 : m + 9] for f in range(5)],
+            [state[f, m + 2 : m + 10] for f in range(5)],
+            2,
+        )
+        for f in range(5):
+            low_y[f, m + 9 : m + 17] = lower[f]
+            high_y[f, m + 9 : m + 17] = upper[f]
+
+    def y_change(f, m):
+        after = high_y[f, m + 8 : m + 16] + low_y[f, m + 9 : m + 17]
+        before = high_y[f, m + 7 : m + 15] + low_y[f, m + 8 : m + 16]
+        return after - before
+
+    def x_sides(state, m):
+        cells = [state[f, m : m + 8] for f in range(5)]
+        lower, upper = cell_sides(
+            [shift_lanes(u, 1) for u in cells], cells, [shift_lanes(u, -1) for u in cells], 1
+        )
+        for f in range(5):
+            low_x[f, m : m + 8] = lower[f]
+            high_x[f, m : m + 8] = upper[f]
+
+    def x_fluxes(f, m):
+        lower = low_x[f, m : m + 8]
+        upper = high_x[f, m : m + 8]
+        return upper + shift_lanes(lower, -1), shift_lanes(upper, 1) + lower
+
+    def y_faces(add):
         for f in range(5):
             for i, m in enumerate((3, 131)):
                 flux = high_y[f, m + 8 : m + 9] + low_y[f, m + 9 : m + 10]
-                if last:
-                    flux = flux + faces_y[i, f : f + 1]
-                faces_y[i, f : f + 1] = flux
-
-    step(state_a, state_b, False)
-    step(state_b, state_a, True)
-
-    pair_index = 2 * (lane & 63)
+                faces_y[i, f : f + 1] = faces_y[i, f : f + 1] + flux if add else flux
+
+    def first_step(m):
+        for f in range(5):
+            after, before = x_fluxes(f, m)
+            faces_x[f, m : m + 8] = jnp.where(lower_face, after, before)
+            state_b[f, m : m + 8] = state_a[f, m : m + 8] - HALF_STEP * ((after - before) + y_change(f, m))
+
+    for m in range(0, 136, 8):
+        y_sides(state_a, m)
+        x_sides(state_a, m)
+    for m in range(0, 136, 8):
+        first_step(m)
+    y_faces(False)
+
+    def second_step_x(m):
+        for f in range(5):
+            after, before = x_fluxes(f, m)
+            faces_x[f, m : m + 8] = faces_x[f, m : m + 8] + jnp.where(lower_face, after, before)
+            change_x[f, m : m + 8] = after - before
+
+    for m in range(0, 136, 8):
+        x_sides(state_b, m)
+    for m in range(0, 136, 8):
+        second_step_x(m)
+    y_sides(state_b, 0)
+    y_sides(state_b, 128)
+    y_faces(True)
+    box_lane = 16 * (lane & 7)
+    face_index = jnp.where((lane & 8) == 0, box_lane + 7, (box_lane + 16) & 127)
+    for k in range(8):
+        m = 4 + 16 * k
+        block = jnp.zeros((8, 128), F32)
+        for f in range(5):
+            pairs = faces_x[f, pl.ds(m, 8, stride=2), :] + faces_x[f, pl.ds(m + 1, 8, stride=2), :]
+            block = jnp.where((lane >> 4) == f, pick_lanes(pairs, face_index), block)
+        face_cols[8 * k : 8 * k + 8] = block
+    face_rows[...] = face_cols[...].T
     for f in range(5):
-        back[f, 0:128] = state_a[f, 4:132].T
-        back[f, 128:136] = back[f, 0:8]
-        for b in range(8):
-            fine_buf[b, f] = back[f, 16 * b + 8 : 16 * b + 16]
-        low = back[f, pl.ds(7, 8, stride=16), :]
-        high = back[f, pl.ds(16, 8, stride=16), :]
-        low = low + shift_lanes(low, -1)
-        high = high + shift_lanes(high, -1)
-        sums_x[pl.ds(f, 8, stride=8), :] = jnp.where(
-            first_lane, pick_lanes(low, pair_index), pick_lanes(high, pair_index)
-        )
-    to_fine = pltpu.make_async_copy(fine_buf, fine_out, out_sem)
+        low = face_rows[16 * f : 16 * f + 8]
+        high = face_rows[16 * f + 8 : 16 * f + 16]
+        sums_x[pl.ds(f, 8, stride=8), :] = jnp.where(first_lane, low, shift_lanes(high, 64))
     low = faces_y[0] + shift_lanes(faces_y[0], -1)
     high = faces_y[1] + shift_lanes(faces_y[1], -1)
     for b in range(8):
@@ -432,9 +479,18 @@
 
     lax.fori_loop(1, GROUP, send_sums, 0)
     pack_sums(0, sum_recv, me)
-    to_fine.start()
-
-    for copy in halo_copies:
+
+    for m in range(8, 128, 8):
+        y_sides(state_b, m)
+    for m in range(0, 136, 8):
+        for f in range(5):
+            state_a[f, m : m + 8] = state_b[f, m : m + 8] - HALF_STEP * (change_x[f, m : m + 8] + y_change(f, m))
+    for f in range(5):
+        back[f] = state_a[f, 4:132].T
+        for b in range(8):
+            fine_out[b, f] = back[f, 16 * b + 8 : 16 * b + 16]
+
+    for copy in halo_copies + edge_copies:
         copy.wait_send()
 
     def wait_sent(o, carry):
@@ -467,11 +523,22 @@
         return carry
 
     lax.fori_loop(1, GROUP, wait_sums_sent, 0)
-    to_fine.wait()
+
+
+def write_out(fine_in, reflux_in, fine_out, reflux_out, sems):
+    copies = [
+        pltpu.make_async_copy(fine_in, fine_out, sems.at[0]),
+        pltpu.make_async_copy(reflux_in, reflux_out, sems.at[1]),
+    ]
+    for copy in copies:
+        copy.start()
+    for copy in copies:
+        copy.wait()
 
 
 def local(previous_fine_boxes, coarse_state, new_source, box_position):
     vmem = pl.BlockSpec(memory_space=pltpu.VMEM)
+    hbm = pl.BlockSpec(memory_space=pltpu.HBM)
     dma = pltpu.SemaphoreType.DMA
     v = pltpu.VMEM
     fine, reflux = pl.pallas_call(
@@ -480,22 +547,25 @@
             jax.ShapeDtypeStruct((8, 5, 8, 128), F32),
             jax.ShapeDtypeStruct((5, 32, 136), F32),
         ),
-        in_specs=[vmem] * 4,
-        out_specs=(pl.BlockSpec(memory_space=pl.ANY), vmem),
+        in_specs=[hbm] * 4,
+        out_specs=(vmem, vmem),
         scratch_shapes=[
+            v((8, 5, 8, 128), F32),
+            v((5, 16, 512), F32),
+            v((8, 128), I32),
+            v((8, 128), I32),
             v((16, 128), I32),
             pltpu.SMEM((16, 128), I32),
             v((40, 48, 128), F32),
-            v((2, 8, 128), F32),
             v((4, 128, 128), F32),
             v((1040, 128), F32),
             v((2, 4, 16, 128), F32),
             v((2, 4, 16, 128), F32),
-            v((6, 8, 128), F32),
+            v((2, 8, 128), F32),
             v((16, 5, 8, 128), F32),
             v((16, 5, 8, 128), F32),
-            v((16, 6, 8, 128), F32),
-            v((16, 6, 8, 128), F32),
+            v((16, 7, 8, 128), F32),
+            v((16, 7, 8, 128), F32),
             v((16, 16, 128), F32),
             v((16, 16, 128), F32),
             v((5, 128, 128), F32),
@@ -507,9 +577,13 @@
             v((5, 160, 128), F32),
             v((5, 160, 128), F32),
             v((5, 136, 128), F32),
+            v((5, 136, 128), F32),
+            v((5, 136, 128), F32),
+            v((5, 152, 128), F32),
             v((2, 8, 128), F32),
-            v((5, 144, 128), F32),
-            v((8, 5, 8, 128), F32),
+            v((128, 128), F32),
+            v((128, 128), F32),
+            v((5, 128, 128), F32),
             v((72, 128), F32),
             v((8, 8, 128), F32),
             v((4, 72, 128), F32),
@@ -519,9 +593,9 @@
             v((192, 128), F32),
             v((192, 128), F32),
             dma,
-            dma,
-            dma((8,)),
-            dma((8,)),
+            dma((4,)),
+            dma((4,)),
+            dma((4,)),
             dma((16,)),
             dma((16,)),
             dma((16,)),
@@ -530,7 +604,7 @@
             dma((16,)),
         ],
         compiler_params=pltpu.CompilerParams(
-            collective_id=0, has_side_effects=True, vmem_limit_bytes=40 * 1024 * 1024
+            collective_id=0, has_side_effects=True, vmem_limit_bytes=64000 * 1024
         ),
     )(
         previous_fine_boxes,
@@ -538,6 +612,16 @@
         new_source.reshape(8, 128),
         box_position.reshape(8, 128),
     )
+    fine, reflux = pl.pallas_call(
+        write_out,
+        out_shape=(
+            jax.ShapeDtypeStruct((8, 5, 8, 128), F32),
+            jax.ShapeDtypeStruct((5, 32, 136), F32),
+        ),
+        in_specs=[vmem] * 2,
+        out_specs=(hbm, hbm),
+        scratch_shapes=[dma((2,))],
+    )(fine, reflux)
     return fine, jnp.transpose(reflux, (1, 0, 2))
 
 

time: 38.4 us -> 30.7 us (0.80)
  local copies, waits for them, and re-layouts: 4.53 us -> 0 us
  Pallas kernels: 33 us -> 29.9 us
    pallas_call x1, Pallas kernels: 33 us -> 28.2 us  [local(): pl.pallas_call(body, out_shape=(jax.ShapeDtypeStruct((8, 5, 8, 128), F32)...]
    unnamed x10 -> x0, local copies, waits for them, and re-layouts: 4.53 us -> none
    pallas_call x0 -> x1, Pallas kernels: none -> 1.73 us  [local(): pl.pallas_call(write_out, out_shape=(jax.ShapeDtypeStruct((8, 5, 8, 128),...]
where the time goes in v2:
time: 30.7 us; the launch traced here: 30.6 us
  Pallas kernels  29.9 us (97%)
  between operations  0.64 us (2%)
    pallas_call x1, Pallas kernels, local(): pl.pallas_call(body, out_shape=(jax.ShapeDtypeStruct((8, 5, 8, 128), F32)...  28.2 us
    pallas_call x1, Pallas kernels, local(): pl.pallas_call(write_out, out_shape=(jax.ShapeDtypeStruct((8, 5, 8, 128),...  1.73 us

profile of v2, /device:TPU:0, one launch (start us, length us, event | category | flops | bytes accessed | tf_op | source)
XLA Modules:
  0.0 30.6 jit_solution(6992154095930632726)
XLA Ops:
  0.6 28.2 %shard_map.59 = (f32[8,5,8,128]{3,2,1,0:T(8,128)}, f32[5,32,136]{2,1,0:T(8,128)}) custom-call(f32[8,5,8,128]{3,2,1,0:T(8,128)} %boxes_in.1, f32[5,16,512]{2,1,0:T(8,128)} %coarse_in.1, s32[8,128]{1,0:T(8,128)} %bitcast.3, s32[8,128]{1,0:T(8,128)} %bitcast.4), custom_call_target="tpu_custom_call" | custom-call | tf_op jit(solution)/shard_map/pallas_call | solution.py:544
  28.9 1.7 %shard_map.60 = (f32[8,5,8,128]{3,2,1,0:T(8,128)}, f32[5,32,136]{2,1,0:T(8,128)}) custom-call(f32[8,5,8,128]{3,2,1,0:T(8,128)} %get-tuple-element.6.fine_in, f32[5,32,136]{2,1,0:T(8,128)} %get-tuple-element.7.reflux_in), custom_call_target="tpu_custom_call" | custom-call | tf_op jit(solution)/shard_map/pallas_call | solution.py:615

commit v3 on v2

--- a/solution.py
+++ b/solution.py
@@ -115,7 +115,7 @@
 
 
 def body(
-    boxes_in, coarse_in, src_in, pos_in, fine_out, reflux_out,
+    boxes_in, coarse_in, maps_in, fine_out, reflux_out,
     boxes, coarse, src_ref, pos_ref, table, tabs, rim, rows_x, cols_x, halo_send, halo_recv, edge_recv,
     box_send, box_recv, ghost_send, ghost_recv, sum_send, sum_recv,
     mixed, turned, coarse_c, coarse_s, state_a, state_b, low_y, high_y, low_x, high_x, change_x, faces_x, faces_y,
@@ -142,8 +142,8 @@
         pl.semaphore_signal(barrier, inc=1, device_id=(gx, peer(o)), device_id_type=MESH)
     fetches = [
         pltpu.make_async_copy(coarse_in, coarse, in_sem.at[0]),
-        pltpu.make_async_copy(src_in, src_ref, in_sem.at[1]),
-        pltpu.make_async_copy(pos_in, pos_ref, in_sem.at[2]),
+        pltpu.make_async_copy(maps_in.at[0], src_ref, in_sem.at[1]),
+        pltpu.make_async_copy(maps_in.at[1], pos_ref, in_sem.at[2]),
         pltpu.make_async_copy(boxes_in, boxes, in_sem.at[3]),
     ]
     for fetch in fetches:
@@ -181,26 +181,50 @@
 
     def box_copy(o):
         return pltpu.make_async_remote_copy(
-            box_send.at[o], box_recv.at[me], box_ss.at[o], box_rs.at[o], (gx, peer(o)), MESH
+            box_send.at[o, pl.ds(0, 50)], box_recv.at[me, pl.ds(0, 50)], box_ss.at[o], box_rs.at[o], (gx, peer(o)), MESH
         )
 
     def ghost_copy(o):
         return pltpu.make_async_remote_copy(
-            ghost_send.at[o], ghost_recv.at[me], ghost_ss.at[o], ghost_rs.at[o], (gx, peer(o)), MESH
+            ghost_send.at[o, pl.ds(0, 44)], ghost_recv.at[me, pl.ds(0, 44)], ghost_ss.at[o], ghost_rs.at[o], (gx, peer(o)), MESH
         )
 
     def sum_copy(o):
         return pltpu.make_async_remote_copy(
-            sum_send.at[o], sum_recv.at[me], sum_ss.at[o], sum_rs.at[o], (gx, peer(o)), MESH
+            sum_send.at[o, pl.ds(0, 15)], sum_recv.at[me, pl.ds(0, 15)], sum_ss.at[o], sum_rs.at[o], (gx, peer(o)), MESH
         )
 
+    first_lane = lane < 64
+
+    def patches(at):
+        spots = [tabs[T_POS, at] & 31, tabs[T_POS + 1, at] & 31]
+        rs = [s >> 3 for s in spots]
+        cs = [s & 7 for s in spots]
+        ids = [(((c & 1) ^ a) * 4 + (c >> 1)) * 5 for a, c in enumerate(cs)]
+        return rs, cs, ids
+
+    def pack_own(at, dest, slot):
+        rs, _, ids = patches(at)
+        for f in range(5):
+            parts = [
+                jnp.where(
+                    sub == 0, rim[ids[a] + f, pl.ds(4 * rs[a] + 8, 8), :], rim[ids[a] + f, pl.ds(4 * rs[a] + 10, 8), :]
+                )
+                for a in range(2)
+            ]
+            dest[slot, 40 + 2 * f : 42 + 2 * f] = jnp.where(first_lane, parts[0], parts[1])[0:2]
+
     def send_box(o, carry):
-        which = tabs[T_BOX, 8 * peer(o)] & 7
-        box_send[o] = boxes[which]
+        at = 8 * peer(o)
+        which = tabs[T_BOX, at] & 7
+        for f in range(5):
+            box_send[o, 8 * f : 8 * f + 8] = boxes[which, f]
+        pack_own(at, box_send, o)
         box_copy(o).start()
         return carry
 
     lax.fori_loop(1, GROUP, send_box, 0)
+    pack_own(8 * me, box_recv, me)
 
     for copy in halo_copies:
         copy.wait_recv()
@@ -225,7 +249,6 @@
     for copy in edge_copies:
         copy.start()
 
-    first_lane = lane < 64
     top_rows = sub < 4
     tenth = jnp.zeros((8, 128), I32)
     for i in range(1, 12):
@@ -234,32 +257,29 @@
 
     def pack_ghosts(o, dest, slot):
         at = 8 * peer(o)
-        spots = [tabs[T_POS, at] & 31, tabs[T_POS + 1, at] & 31]
-        rs = [s >> 3 for s in spots]
-        cs = [s & 7 for s in spots]
-        ids = [(((c & 1) ^ a) * 4 + (c >> 1)) * 5 for a, c in enumerate(cs)]
+        rs, cs, ids = patches(at)
         for f in range(5):
             parts = [
                 jnp.where(
-                    top_rows, rim[ids[a] + f, pl.ds(4 * rs[a] + 5, 8), :], rim[ids[a] + f, pl.ds(4 * rs[a] + 7, 8), :]
+                    sub < 3, rim[ids[a] + f, pl.ds(4 * rs[a] + 5, 8), :], rim[ids[a] + f, pl.ds(4 * rs[a] + 9, 8), :]
                 )
                 for a in range(2)
             ]
-            dest[slot, f] = jnp.where(first_lane, parts[0], parts[1])
+            dest[slot, 6 * f : 6 * f + 6] = jnp.where(first_lane, parts[0], parts[1])[0:6]
         sides = []
         for a in range(2):
             strip = jnp.where(
                 top_rows, cols_x[pl.ds(64 * cs[a] + 5, 8), :], cols_x[pl.ds(64 * cs[a] + 67, 8), :]
             )
             sides.append(pick_lanes(strip, side_index + 4 * rs[a]))
-        dest[slot, 5] = jnp.where(lane < 50, sides[0], sides[1])
-        edge = jnp.where(top_rows, cols_x[517:525], cols_x[3:11])
+        dest[slot, 30:38] = jnp.where(lane < 50, sides[0], sides[1])
+        edge = jnp.where(sub < 3, cols_x[517:525], cols_x[5:13])
         edges = []
         for a in range(2):
             low = (tabs[T_POS_NEXT + a, at] & 31) >> 3
             high = (tabs[T_POS_BEFORE + a, at] & 31) >> 3
-            edges.append(pick_lanes(edge, side_index + 4 * jnp.where(top_rows, low, high)))
-        dest[slot, 6] = jnp.where(lane < 50, edges[0], edges[1])
+            edges.append(pick_lanes(edge, side_index + 4 * jnp.where(sub < 3, low, high)))
+        dest[slot, 38:44] = jnp.where(lane < 50, edges[0], edges[1])[0:6]
 
     def send_ghosts(o, carry):
         pack_ghosts(o, ghost_send, o)
@@ -315,8 +335,6 @@
         return carry
 
     lax.fori_loop(1, GROUP, wait_boxes, 0)
-    lax.fori_loop(1, GROUP, wait_ghosts, 0)
-    side_parts = [jnp.zeros((8, 128), F32) for _ in range(5)]
     for b in range(8):
         at = 8 * me + b
         device = tabs[T_DEV, at] & 15
@@ -325,15 +343,23 @@
         second = tabs[T_RANK, at] == 1
         stays = device == me
         for f in range(5):
-            box = jnp.where(stays, boxes[local, f], box_recv[device, f])
-            inner = ghost_recv[owner, f]
-            inner = jnp.where(second, shift_lanes(inner, 64), inner)
-            mixed[f, 16 * b : 16 * b + 8] = inner
+            box = jnp.where(stays, boxes[local, f], box_recv[device, 8 * f : 8 * f + 8])
             mixed[f, 16 * b + 8 : 16 * b + 16] = box
+            own = box_recv[owner, 40 + 2 * f : 42 + 2 * f]
+            mixed[f, 16 * b + 6 : 16 * b + 8] = jnp.where(second, pltpu.roll(own, 64, axis=1), own)
+    lax.fori_loop(1, GROUP, wait_ghosts, 0)
+    side_parts = [jnp.zeros((8, 128), F32) for _ in range(5)]
+    for b in range(8):
+        at = 8 * me + b
+        owner = tabs[T_OWN, at] & 15
+        second = tabs[T_RANK, at] == 1
+        for f in range(5):
+            inner = ghost_recv[owner, 6 * f : 6 * f + 8]
+            mixed[f, 16 * b : 16 * b + 6] = jnp.where(second, shift_lanes(inner, 64), inner)[0:6]
         column = tabs[T_SPOT, at] & 7
-        low_edge = ghost_recv[(owner + 15) & 15, 6]
-        high_edge = ghost_recv[(owner + 1) & 15, 6]
-        side = ghost_recv[owner, 5]
+        low_edge = ghost_recv[(owner + 15) & 15, 38:46]
+        high_edge = ghost_recv[(owner + 1) & 15, 36:44]
+        side = ghost_recv[owner, 30:38]
         side = jnp.where((sub < 3) & (column == 0), low_edge, side)
         side = jnp.where((sub >= 5) & (column == 7), high_edge, side)
         side = jnp.where(second, shift_lanes(side, -50), side)
@@ -346,7 +372,7 @@
     coarse_row = (row >> 1) + 1
 
     def kept(i):
-        return jnp.where(i < 4, i, jnp.where(i < 6, 3, i - 2))
+        return jnp.where(i < 3, i, jnp.where(i < 6, 6, jnp.where(i == 6, 7, i - 4)))
 
     inner_index = [base + kept(coarse_row + d) for d in (0, -1, 1)]
     side_rows = [base + coarse_row + d for d in (0, -1, 1)]
@@ -547,7 +573,7 @@
             jax.ShapeDtypeStruct((8, 5, 8, 128), F32),
             jax.ShapeDtypeStruct((5, 32, 136), F32),
         ),
-        in_specs=[hbm] * 4,
+        in_specs=[hbm] * 3,
         out_specs=(vmem, vmem),
         scratch_shapes=[
             v((8, 5, 8, 128), F32),
@@ -562,10 +588,10 @@
             v((2, 4, 16, 128), F32),
             v((2, 4, 16, 128), F32),
             v((2, 8, 128), F32),
-            v((16, 5, 8, 128), F32),
-            v((16, 5, 8, 128), F32),
-            v((16, 7, 8, 128), F32),
-            v((16, 7, 8, 128), F32),
+            v((16, 56, 128), F32),
+            v((16, 56, 128), F32),
+            v((16, 48, 128), F32),
+            v((16, 48, 128), F32),
             v((16, 16, 128), F32),
             v((16, 16, 128), F32),
             v((5, 128, 128), F32),
@@ -604,13 +630,12 @@
             dma((16,)),
         ],
         compiler_params=pltpu.CompilerParams(
-            collective_id=0, has_side_effects=True, vmem_limit_bytes=64000 * 1024
+            collective_id=0, has_side_effects=True, vmem_limit_bytes=54880 * 1024
         ),
     )(
         previous_fine_boxes,
         coarse_state,
-        new_source.reshape(8, 128),
-        box_position.reshape(8, 128),
+        jnp.stack([new_source.reshape(8, 128), box_position.reshape(8, 128)]),
     )
     fine, reflux = pl.pallas_call(
         write_out,
@@ -621,6 +646,7 @@
         in_specs=[vmem] * 2,
         out_specs=(hbm, hbm),
         scratch_shapes=[dma((2,))],
+        compiler_params=pltpu.CompilerParams(vmem_limit_bytes=1024 * 1024),
     )(fine, reflux)
     return fine, jnp.transpose(reflux, (1, 0, 2))
 

time: 30.7 us -> 28.6 us (0.932)
  Pallas kernels: 29.9 us -> 27.1 us
  other arithmetic: 0 us -> 0.71 us
    pallas_call x1, Pallas kernels: 28.2 us -> 26.4 us  [local(): pl.pallas_call(body, out_shape=(jax.ShapeDtypeStruct((8, 5, 8, 128), F32)...]
    pallas_call x1, Pallas kernels: 1.73 us -> 0.74 us  [local(): pl.pallas_call(write_out, out_shape=(jax.ShapeDtypeStruct((8, 5, 8, 128),...]
    another operation x0 -> x1, other arithmetic: none -> 0.71 us  [local(): jnp.stack([new_source.reshape(8, 128), box_position.reshape(8, 128)])]
where the time goes in v3:
time: 28.6 us; the launch traced here: 28.5 us
  Pallas kernels  27.1 us (95%)
  other arithmetic  0.71 us (2%)
  between operations  0.64 us (2%)
    pallas_call x1, Pallas kernels, local(): pl.pallas_call(body, out_shape=(jax.ShapeDtypeStruct((8, 5, 8, 128), F32)...  26.4 us
    pallas_call x1, Pallas kernels, local(): pl.pallas_call(write_out, out_shape=(jax.ShapeDtypeStruct((8, 5, 8, 128),...  0.74 us
    another operation x1, other arithmetic, local(): jnp.stack([new_source.reshape(8, 128), box_position.reshape(8, 128)])  0.71 us

profile of v3, /device:TPU:0, one launch (start us, length us, event | category | flops | bytes accessed | tf_op | source)
XLA Modules:
  0.0 28.5 jit_solution(14757629704004149054)
XLA Ops:
  0.6 0.7 %pad_add_fusion.maps_in = s32[2,8,128]{2,1,0:T(8,128)S(1)} fusion(s32[1,8,128]{2,1,0:T(8,128)} %bitcast.3, s32[1,8,128]{2,1,0:T(8,128)} %bitcast.4), kind=kLoop, calls=%fused_computation | loop fusion | flops 2048 | bytes 16384 | tf_op jit(solution)/shard_map/stack | solution.py:638
  1.3 26.4 %shard_map.59 = (f32[8,5,8,128]{3,2,1,0:T(8,128)S(1)}, f32[5,32,136]{2,1,0:T(8,128)S(1)}) custom-call(f32[8,5,8,128]{3,2,1,0:T(8,128)} %boxes_in.1, f32[5,16,512]{2,1,0:T(8,128)} %coarse_in.1, s32[2,8,128]{2,1,0:T(8,128)S(1)} %pad_add_fusion.maps_in), custom_call_target="tpu_custom_call" | custom-call | tf_op jit(solution)/shard_map/pallas_call | solution.py:570
  27.7 0.7 %shard_map.60 = (f32[8,5,8,128]{3,2,1,0:T(8,128)}, f32[5,32,136]{2,1,0:T(8,128)}) custom-call(f32[8,5,8,128]{3,2,1,0:T(8,128)S(1)} %get-tuple-element.6.fine_in, f32[5,32,136]{2,1,0:T(8,128)S(1)} %get-tuple-element.7.reflux_in), custom_call_target="tpu_custom_call" | custom-call | tf_op jit(solution)/shard_map/pallas_call | solution.py:640

commit v4 on v3

--- a/solution.py
+++ b/solution.py
@@ -68,11 +68,11 @@
     return [u + l for u, l in zip(upper, lower)]
 
 
-def make_tables(src_ref, pos_ref, gx, me, table):
+def make_tables(maps, gx, me, table):
     lane = iota(1)
     sub = iota(0)
-    src = jnp.broadcast_to(src_ref[pl.ds(gx, 1), :], (8, 128)) & 127
-    pos = jnp.broadcast_to(pos_ref[pl.ds(gx, 1), :], (8, 128)) & 511
+    src = jnp.broadcast_to(maps[0, pl.ds(gx, 1), :], (8, 128)) & 127
+    pos = jnp.broadcast_to(maps[1, pl.ds(gx, 1), :], (8, 128)) & 511
     place = pick_lanes(pos, src)
     device = src >> 3
     local = src & 7
@@ -116,11 +116,12 @@
 
 def body(
     boxes_in, coarse_in, maps_in, fine_out, reflux_out,
-    boxes, coarse, src_ref, pos_ref, table, tabs, rim, rows_x, cols_x, halo_send, halo_recv, edge_recv,
+    boxes, coarse, maps, table, tabs, rim, rows_x, cols_x, halo_send, halo_recv, edge_send, edge_recv,
     box_send, box_recv, ghost_send, ghost_recv, sum_send, sum_recv,
     mixed, turned, coarse_c, coarse_s, state_a, state_b, low_y, high_y, low_x, high_x, change_x, faces_x, faces_y,
     face_cols, face_rows, back, sums_x, sums_y, line_x, line_y, own_x, own_y, out_x, out_y,
-    table_sem, in_sem, halo_ss, halo_rs, box_ss, box_rs, ghost_ss, ghost_rs, sum_ss, sum_rs,
+    table_sem, coarse_sem, maps_sem, boxes_sem, halo_ss, halo_rs, edge_ss, edge_rs,
+    box_ss, box_rs, ghost_ss, ghost_rs, sum_ss, sum_rs,
 ):
     gx = lax.axis_index("gx")
     me = lax.axis_index("gy")
@@ -141,17 +142,15 @@
     for o in (1, 15, 4, 12, 2, 14, 8, 3, 13, 5, 11, 6, 10, 7, 9):
         pl.semaphore_signal(barrier, inc=1, device_id=(gx, peer(o)), device_id_type=MESH)
     fetches = [
-        pltpu.make_async_copy(coarse_in, coarse, in_sem.at[0]),
-        pltpu.make_async_copy(maps_in.at[0], src_ref, in_sem.at[1]),
-        pltpu.make_async_copy(maps_in.at[1], pos_ref, in_sem.at[2]),
-        pltpu.make_async_copy(boxes_in, boxes, in_sem.at[3]),
+        pltpu.make_async_copy(coarse_in, coarse, coarse_sem),
+        pltpu.make_async_copy(maps_in, maps, maps_sem),
+        pltpu.make_async_copy(boxes_in, boxes, boxes_sem),
     ]
     for fetch in fetches:
         fetch.start()
 
     fetches[1].wait()
-    fetches[2].wait()
-    make_tables(src_ref, pos_ref, gx, me, table)
+    make_tables(maps, gx, me, table)
     to_scalars = pltpu.make_async_copy(table, tabs, table_sem)
     to_scalars.start()
 
@@ -166,33 +165,30 @@
             rows_x[t, 22 * f + 3 : 22 * f + 19] = tile
 
     pl.semaphore_wait(barrier, GROUP + 1)
-    halo_copies = []
+    def halo_copy(part, there):
+        return pltpu.make_async_remote_copy(
+            halo_send.at[part], halo_recv.at[part], halo_ss, halo_rs, there, MESH
+        )
+
     for i, there in enumerate(near):
-        halo_copies.append(
-            pltpu.make_async_remote_copy(
-                halo_send.at[i], halo_recv.at[i], halo_ss.at[i], halo_rs.at[i], there, MESH
-            )
+        halo_copy(i, there).start()
+    both_halos = halo_copy(pl.ds(0, 2), near[0])
+
+    to_scalars.wait()
+    fetches[2].wait()
+
+    def group_copy(source, target, rows, sems, o):
+        return pltpu.make_async_remote_copy(
+            source.at[o, pl.ds(0, rows)], target.at[me, pl.ds(0, rows)], *sems, (gx, peer(o)), MESH
         )
-    for copy in halo_copies:
-        copy.start()
-
-    to_scalars.wait()
-    fetches[3].wait()
-
-    def box_copy(o):
-        return pltpu.make_async_remote_copy(
-            box_send.at[o, pl.ds(0, 50)], box_recv.at[me, pl.ds(0, 50)], box_ss.at[o], box_rs.at[o], (gx, peer(o)), MESH
-        )
-
-    def ghost_copy(o):
-        return pltpu.make_async_remote_copy(
-            ghost_send.at[o, pl.ds(0, 44)], ghost_recv.at[me, pl.ds(0, 44)], ghost_ss.at[o], ghost_rs.at[o], (gx, peer(o)), MESH
-        )
-
-    def sum_copy(o):
-        return pltpu.make_async_remote_copy(
-            sum_send.at[o, pl.ds(0, 15)], sum_recv.at[me, pl.ds(0, 15)], sum_ss.at[o], sum_rs.at[o], (gx, peer(o)), MESH
-        )
+
+    def whole_copy(source, target, rows, sems):
+        parts = (pl.ds(0, GROUP - 1), pl.ds(0, rows))
+        return pltpu.make_async_remote_copy(source.at[parts], target.at[parts], *sems, (gx, peer(1)), MESH)
+
+    box_args = (box_send, box_recv, 50, (box_ss, box_rs))
+    ghost_args = (ghost_send, ghost_recv, 44, (ghost_ss, ghost_rs))
+    sum_args = (sum_send, sum_recv, 11, (sum_ss, sum_rs))
 
     first_lane = lane < 64
 
@@ -220,14 +216,13 @@
         for f in range(5):
             box_send[o, 8 * f : 8 * f + 8] = boxes[which, f]
         pack_own(at, box_send, o)
-        box_copy(o).start()
+        group_copy(*box_args, o).start()
         return carry
 
     lax.fori_loop(1, GROUP, send_box, 0)
     pack_own(8 * me, box_recv, me)
 
-    for copy in halo_copies:
-        copy.wait_recv()
+    both_halos.wait_recv()
     for t in range(4):
         for f in range(5):
             top = halo_recv[0, t, 3 * f : 3 * f + 3]
@@ -240,14 +235,15 @@
             rows_x[t, 22 * f + 19 : 22 * f + 22] = bottom
     for t in range(4):
         cols_x[8 + 128 * t : 136 + 128 * t] = rows_x[t].T
-    edge_copies = [
-        pltpu.make_async_remote_copy(
-            cols_x.at[pl.ds(at, 8)], edge_recv.at[i], halo_ss.at[2 + i], halo_rs.at[2 + i], there, MESH
+    def edge_copy(part, there):
+        return pltpu.make_async_remote_copy(
+            edge_send.at[part], edge_recv.at[part], edge_ss, edge_rs, there, MESH
         )
-        for i, (at, there) in enumerate(zip((8, 512), beside))
-    ]
-    for copy in edge_copies:
-        copy.start()
+
+    for i, (at, there) in enumerate(zip((8, 512), beside)):
+        edge_send[i] = cols_x[at : at + 8]
+        edge_copy(i, there).start()
+    both_edges = edge_copy(pl.ds(0, 2), beside[0])
 
     top_rows = sub < 4
     tenth = jnp.zeros((8, 128), I32)
@@ -283,7 +279,7 @@
 
     def send_ghosts(o, carry):
         pack_ghosts(o, ghost_send, o)
-        ghost_copy(o).start()
+        group_copy(*ghost_args, o).start()
         return carry
 
     lax.fori_loop(1, GROUP, send_ghosts, 0)
@@ -297,8 +293,7 @@
         flux = interface_flux(cells, 1)
         for f in range(5):
             line_x[t, pl.ds(f, 8, stride=8), :] = flux[f]
-    for copy in edge_copies:
-        copy.wait_recv()
+    both_edges.wait_recv()
     cols_x[0:8] = edge_recv[1]
     cols_x[520:528] = edge_recv[0]
     for f5 in range(2):
@@ -326,15 +321,7 @@
                 lane < 4, shift_lanes(low, -4 * r), shift_lanes(high, 4 - 4 * r)
             )
 
-    def wait_boxes(o, carry):
-        box_copy(o).wait_recv()
-        return carry
-
-    def wait_ghosts(o, carry):
-        ghost_copy(o).wait_recv()
-        return carry
-
-    lax.fori_loop(1, GROUP, wait_boxes, 0)
+    whole_copy(*box_args).wait_recv()
     for b in range(8):
         at = 8 * me + b
         device = tabs[T_DEV, at] & 15
@@ -347,7 +334,7 @@
             mixed[f, 16 * b + 8 : 16 * b + 16] = box
             own = box_recv[owner, 40 + 2 * f : 42 + 2 * f]
             mixed[f, 16 * b + 6 : 16 * b + 8] = jnp.where(second, pltpu.roll(own, 64, axis=1), own)
-    lax.fori_loop(1, GROUP, wait_ghosts, 0)
+    whole_copy(*ghost_args).wait_recv()
     side_parts = [jnp.zeros((8, 128), F32) for _ in range(5)]
     for b in range(8):
         at = 8 * me + b
@@ -482,9 +469,11 @@
         sums_x[pl.ds(f, 8, stride=8), :] = jnp.where(first_lane, low, shift_lanes(high, 64))
     low = faces_y[0] + shift_lanes(faces_y[0], -1)
     high = faces_y[1] + shift_lanes(faces_y[1], -1)
+    field = jnp.where(lane < 40, lane >> 3, (lane >> 3) - 5)
     for b in range(8):
         index = 16 * b + 8 + 2 * (lane & 3)
-        sums_y[b] = jnp.where((lane & 4) == 0, pick_lanes(low, index), pick_lanes(high, index))
+        both = jnp.where((lane & 4) == 0, pick_lanes(low, index), pick_lanes(high, index))
+        sums_y[b : b + 1] = jnp.sum(jnp.where(sub == field, both, 0.0), axis=0, keepdims=True)
 
     def pack_sums(o, dest, slot):
         at = 8 * peer(o)
@@ -492,15 +481,11 @@
         second = tabs[T_BACK + 1, at] & 7
         dest[slot, 0:8] = sums_x[pl.ds(8 * first, 8), :]
         dest[slot, 5:13] = sums_x[pl.ds(8 * second, 8), :]
-        dest[slot, 10:16] = jnp.where(lane < 8, sums_y[first], sums_y[second])[0:6]
+        dest[slot, 10:11] = jnp.where(lane[0:1] < 40, sums_y[pl.ds(first, 1)], sums_y[pl.ds(second, 1)])
 
     def send_sums(o, carry):
         pack_sums(o, sum_send, o)
-        sum_copy(o).start()
-        return carry
-
-    def wait_sums(o, carry):
-        sum_copy(o).wait_recv()
+        group_copy(*sum_args, o).start()
         return carry
 
     lax.fori_loop(1, GROUP, send_sums, 0)
@@ -516,39 +501,30 @@
         for b in range(8):
             fine_out[b, f] = back[f, 16 * b + 8 : 16 * b + 16]
 
-    for copy in halo_copies + edge_copies:
-        copy.wait_send()
-
-    def wait_sent(o, carry):
-        box_copy(o).wait_send()
-        ghost_copy(o).wait_send()
-        return carry
-
-    lax.fori_loop(1, GROUP, wait_sent, 0)
-    lax.fori_loop(1, GROUP, wait_sums, 0)
+    both_halos.wait_send()
+    both_edges.wait_send()
+    whole_copy(*box_args).wait_send()
+    whole_copy(*ghost_args).wait_send()
+    whole_copy(*sum_args).wait_recv()
 
     sign_x = jnp.where(first_lane, SUM_SCALE, -SUM_SCALE)
+    sign_y = jnp.where(lane < 4, SUM_SCALE, -SUM_SCALE)
+    y_index = 8 * jnp.minimum(sub, 4) + (lane & 7)
     for n in range(32):
         entry = tabs[T_INV, n]
         live = entry > 0
         slot = (entry - 1) & 31
         sender = slot >> 1
-        second = (slot & 1) == 1
         total_x = sum_recv[sender, pl.ds(5 * (slot & 1), 8), :]
-        total_y = sum_recv[sender, pl.ds(10, 6), :]
-        total_y = jnp.where(second, pltpu.roll(total_y, 120, axis=1), total_y)
-        sign_y = jnp.where(lane[0:5] < 4, SUM_SCALE, -SUM_SCALE)
+        total_y = jnp.broadcast_to(sum_recv[sender, 10:11], (8, 128))
+        total_y = pick_lanes(total_y, y_index + 40 * (slot & 1))
         out_x[pl.ds(n, 5, stride=32), :] = jnp.where(live, own_x[n, 0:5] - sign_x[0:5] * total_x[0:5], 0.0)
-        out_y[pl.ds(n, 5, stride=32), :] = jnp.where(live, own_y[n, 0:5] - sign_y * total_y[0:5], 0.0)
+        out_y[pl.ds(n, 5, stride=32), :] = jnp.where(live, own_y[n, 0:5] - sign_y[0:5] * total_y[0:5], 0.0)
     for f in range(5):
         reflux_out[f, :, 0:128] = out_x[32 * f : 32 * f + 32]
         reflux_out[f, :, 128:136] = out_y[32 * f : 32 * f + 32][:, 0:8]
 
-    def wait_sums_sent(o, carry):
-        sum_copy(o).wait_send()
-        return carry
-
-    lax.fori_loop(1, GROUP, wait_sums_sent, 0)
+    whole_copy(*sum_args).wait_send()
 
 
 def write_out(fine_in, reflux_in, fine_out, reflux_out, sems):
@@ -578,8 +554,7 @@
         scratch_shapes=[
             v((8, 5, 8, 128), F32),
             v((5, 16, 512), F32),
-            v((8, 128), I32),
-            v((8, 128), I32),
+            v((2, 8, 128), I32),
             v((16, 128), I32),
             pltpu.SMEM((16, 128), I32),
             v((40, 48, 128), F32),
@@ -587,6 +562,7 @@
             v((1040, 128), F32),
             v((2, 4, 16, 128), F32),
             v((2, 4, 16, 128), F32),
+            v((2, 8, 128), F32),
             v((2, 8, 128), F32),
             v((16, 56, 128), F32),
             v((16, 56, 128), F32),
@@ -611,23 +587,14 @@
             v((128, 128), F32),
             v((5, 128, 128), F32),
             v((72, 128), F32),
-            v((8, 8, 128), F32),
+            v((8, 128), F32),
             v((4, 72, 128), F32),
             v((136, 128), F32),
             v((32, 8, 128), F32),
             v((32, 8, 128), F32),
             v((192, 128), F32),
             v((192, 128), F32),
-            dma,
-            dma((4,)),
-            dma((4,)),
-            dma((4,)),
-            dma((16,)),
-            dma((16,)),
-            dma((16,)),
-            dma((16,)),
-            dma((16,)),
-            dma((16,)),
+            *[dma] * 14,
         ],
         compiler_params=pltpu.CompilerParams(
             collective_id=0, has_side_effects=True, vmem_limit_bytes=54880 * 1024

time: 28.6 us -> 27.5 us (0.962)
  Pallas kernels: 27.1 us -> 26 us
    pallas_call x1, Pallas kernels: 26.4 us -> 25.2 us  [local(): pl.pallas_call(body, out_shape=(jax.ShapeDtypeStruct((8, 5, 8, 128), F32)...]
where the time goes in v4:
time: 27.5 us; the launch traced here: 27.3 us
  Pallas kernels  26 us (95%)
  other arithmetic  0.71 us (3%)
  between operations  0.64 us (2%)
    pallas_call x1, Pallas kernels, local(): pl.pallas_call(body, out_shape=(jax.ShapeDtypeStruct((8, 5, 8, 128), F32)...  25.2 us
    pallas_call x1, Pallas kernels, local(): pl.pallas_call(write_out, out_shape=(jax.ShapeDtypeStruct((8, 5, 8, 128),...  0.74 us
    another operation x1, other arithmetic, local(): jnp.stack([new_source.reshape(8, 128), box_position.reshape(8, 128)])  0.71 us

profile of v4, /device:TPU:0, one launch (start us, length us, event | category | flops | bytes accessed | tf_op | source)
XLA Modules:
  0.0 27.3 jit_solution(1564773822301719241)
XLA Ops:
  0.6 0.7 %pad_add_fusion.maps_in = s32[2,8,128]{2,1,0:T(8,128)S(1)} fusion(s32[1,8,128]{2,1,0:T(8,128)} %bitcast.3, s32[1,8,128]{2,1,0:T(8,128)} %bitcast.4), kind=kLoop, calls=%fused_computation | loop fusion | flops 2048 | bytes 16384 | tf_op jit(solution)/shard_map/stack | solution.py:605
  1.3 25.2 %shard_map.59 = (f32[8,5,8,128]{3,2,1,0:T(8,128)S(1)}, f32[5,32,136]{2,1,0:T(8,128)S(1)}) custom-call(f32[8,5,8,128]{3,2,1,0:T(8,128)} %boxes_in.1, f32[5,16,512]{2,1,0:T(8,128)} %coarse_in.1, s32[2,8,128]{2,1,0:T(8,128)S(1)} %pad_add_fusion.maps_in), custom_call_target="tpu_custom_call" | custom-call | tf_op jit(solution)/shard_map/pallas_call | solution.py:546
  26.6 0.7 %shard_map.60 = (f32[8,5,8,128]{3,2,1,0:T(8,128)}, f32[5,32,136]{2,1,0:T(8,128)}) custom-call(f32[8,5,8,128]{3,2,1,0:T(8,128)S(1)} %get-tuple-element.6.fine_in, f32[5,32,136]{2,1,0:T(8,128)S(1)} %get-tuple-element.7.reflux_in), custom_call_target="tpu_custom_call" | custom-call | tf_op jit(solution)/shard_map/pallas_call | solution.py:607

commit v5 on v4

--- a/solution.py
+++ b/solution.py
@@ -164,31 +164,8 @@
             rim[20 + t * 5 + f, 8:24] = pltpu.roll(tile, 64, axis=1)
             rows_x[t, 22 * f + 3 : 22 * f + 19] = tile
 
-    pl.semaphore_wait(barrier, GROUP + 1)
-    def halo_copy(part, there):
-        return pltpu.make_async_remote_copy(
-            halo_send.at[part], halo_recv.at[part], halo_ss, halo_rs, there, MESH
-        )
-
-    for i, there in enumerate(near):
-        halo_copy(i, there).start()
-    both_halos = halo_copy(pl.ds(0, 2), near[0])
-
     to_scalars.wait()
     fetches[2].wait()
-
-    def group_copy(source, target, rows, sems, o):
-        return pltpu.make_async_remote_copy(
-            source.at[o, pl.ds(0, rows)], target.at[me, pl.ds(0, rows)], *sems, (gx, peer(o)), MESH
-        )
-
-    def whole_copy(source, target, rows, sems):
-        parts = (pl.ds(0, GROUP - 1), pl.ds(0, rows))
-        return pltpu.make_async_remote_copy(source.at[parts], target.at[parts], *sems, (gx, peer(1)), MESH)
-
-    box_args = (box_send, box_recv, 50, (box_ss, box_rs))
-    ghost_args = (ghost_send, ghost_recv, 44, (ghost_ss, ghost_rs))
-    sum_args = (sum_send, sum_recv, 11, (sum_ss, sum_rs))
 
     first_lane = lane < 64
 
@@ -210,12 +187,40 @@
             ]
             dest[slot, 40 + 2 * f : 42 + 2 * f] = jnp.where(first_lane, parts[0], parts[1])[0:2]
 
-    def send_box(o, carry):
+    def pack_box(o, carry):
         at = 8 * peer(o)
         which = tabs[T_BOX, at] & 7
         for f in range(5):
             box_send[o, 8 * f : 8 * f + 8] = boxes[which, f]
         pack_own(at, box_send, o)
+        return carry
+
+    lax.fori_loop(1, GROUP, pack_box, 0)
+    pl.semaphore_wait(barrier, GROUP + 1)
+    def halo_copy(part, there):
+        return pltpu.make_async_remote_copy(
+            halo_send.at[part], halo_recv.at[part], halo_ss, halo_rs, there, MESH
+        )
+
+    for i, there in enumerate(near):
+        halo_copy(i, there).start()
+    both_halos = halo_copy(pl.ds(0, 2), near[0])
+
+
+    def group_copy(source, target, rows, sems, o):
+        return pltpu.make_async_remote_copy(
+            source.at[o, pl.ds(0, rows)], target.at[me, pl.ds(0, rows)], *sems, (gx, peer(o)), MESH
+        )
+
+    def whole_copy(source, target, rows, sems):
+        parts = (pl.ds(0, GROUP - 1), pl.ds(0, rows))
+        return pltpu.make_async_remote_copy(source.at[parts], target.at[parts], *sems, (gx, peer(1)), MESH)
+
+    box_args = (box_send, box_recv, 50, (box_ss, box_rs))
+    ghost_args = (ghost_send, ghost_recv, 44, (ghost_ss, ghost_rs))
+    sum_args = (sum_send, sum_recv, 11, (sum_ss, sum_rs))
+
+    def send_box(o, carry):
         group_copy(*box_args, o).start()
         return carry
 

time: 27.5 us -> 27.5 us (level)
  no operation moved by 1% of the time
where the time goes in v5:
time: 27.5 us; the launch traced here: 27.3 us
  Pallas kernels  26 us (95%)
  other arithmetic  0.71 us (3%)
  between operations  0.64 us (2%)
    pallas_call x1, Pallas kernels, local(): pl.pallas_call(body, out_shape=(jax.ShapeDtypeStruct((8, 5, 8, 128), F32)...  25.2 us
    pallas_call x1, Pallas kernels, local(): pl.pallas_call(write_out, out_shape=(jax.ShapeDtypeStruct((8, 5, 8, 128),...  0.74 us
    another operation x1, other arithmetic, local(): jnp.stack([new_source.reshape(8, 128), box_position.reshape(8, 128)])  0.71 us

profile of v5, /device:TPU:0, one launch (start us, length us, event | category | flops | bytes accessed | tf_op | source)
XLA Modules:
  0.0 27.3 jit_solution(255755820421725390)
XLA Ops:
  0.6 0.7 %pad_add_fusion.maps_in = s32[2,8,128]{2,1,0:T(8,128)S(1)} fusion(s32[1,8,128]{2,1,0:T(8,128)} %bitcast.3, s32[1,8,128]{2,1,0:T(8,128)} %bitcast.4), kind=kLoop, calls=%fused_computation | loop fusion | flops 2048 | bytes 16384 | tf_op jit(solution)/shard_map/stack | solution.py:610
  1.3 25.2 %shard_map.59 = (f32[8,5,8,128]{3,2,1,0:T(8,128)S(1)}, f32[5,32,136]{2,1,0:T(8,128)S(1)}) custom-call(f32[8,5,8,128]{3,2,1,0:T(8,128)} %boxes_in.1, f32[5,16,512]{2,1,0:T(8,128)} %coarse_in.1, s32[2,8,128]{2,1,0:T(8,128)S(1)} %pad_add_fusion.maps_in), custom_call_target="tpu_custom_call" | custom-call | tf_op jit(solution)/shard_map/pallas_call | solution.py:551
  26.6 0.7 %shard_map.60 = (f32[8,5,8,128]{3,2,1,0:T(8,128)}, f32[5,32,136]{2,1,0:T(8,128)}) custom-call(f32[8,5,8,128]{3,2,1,0:T(8,128)S(1)} %get-tuple-element.6.fine_in, f32[5,32,136]{2,1,0:T(8,128)S(1)} %get-tuple-element.7.reflux_in), custom_call_target="tpu_custom_call" | custom-call | tf_op jit(solution)/shard_map/pallas_call | solution.py:612

commit v6 on v4

--- a/solution.py
+++ b/solution.py
@@ -11,6 +11,7 @@
 
 GROUP = 16
 SLABS = 8
+BOXES = 1024
 GAMMA_LESS = 0.4
 STEP_RATIO = 0.15
 WAVE_SPEED = 2.5
@@ -71,8 +72,9 @@
 def make_tables(maps, gx, me, table):
     lane = iota(1)
     sub = iota(0)
-    src = jnp.broadcast_to(maps[0, pl.ds(gx, 1), :], (8, 128)) & 127
-    pos = jnp.broadcast_to(maps[1, pl.ds(gx, 1), :], (8, 128)) & 511
+    both = jnp.broadcast_to(maps[pl.ds(gx, 1), :], (8, 128))
+    src = both & 127
+    pos = (both >> 10) & 511
     place = pick_lanes(pos, src)
     device = src >> 3
     local = src & 7
@@ -554,7 +556,7 @@
         scratch_shapes=[
             v((8, 5, 8, 128), F32),
             v((5, 16, 512), F32),
-            v((2, 8, 128), I32),
+            v((8, 128), I32),
             v((16, 128), I32),
             pltpu.SMEM((16, 128), I32),
             v((40, 48, 128), F32),
@@ -602,7 +604,7 @@
     )(
         previous_fine_boxes,
         coarse_state,
-        jnp.stack([new_source.reshape(8, 128), box_position.reshape(8, 128)]),
+        (new_source + BOXES * box_position).reshape(8, 128),
     )
     fine, reflux = pl.pallas_call(
         write_out,

time: 27.5 us -> 27.6 us (level)
    reshape x0 -> x1, other arithmetic: none -> 0.71 us  [local(): (new_source + BOXES * box_position).reshape(8, 128)]
    another operation x1 -> x0, other arithmetic: 0.71 us -> none  [local(): jnp.stack([new_source.reshape(8, 128), box_position.reshape(8, 128)])]
where the time goes in v6:
time: 27.6 us; the launch traced here: 27.3 us
  Pallas kernels  26 us (94%)
  other arithmetic  0.71 us (3%)
  between operations  0.64 us (2%)
    pallas_call x1, Pallas kernels, local(): pl.pallas_call(body, out_shape=(jax.ShapeDtypeStruct((8, 5, 8, 128), F32)...  25.3 us
    pallas_call x1, Pallas kernels, local(): pl.pallas_call(write_out, out_shape=(jax.ShapeDtypeStruct((8, 5, 8, 128),...  0.74 us
    reshape x1, other arithmetic, local(): (new_source + BOXES * box_position).reshape(8, 128)  0.71 us

profile of v6, /device:TPU:0, one launch (start us, length us, event | category | flops | bytes accessed | tf_op | source)
XLA Modules:
  0.0 27.3 jit_solution(16122832673871337394)
XLA Ops:
  0.6 0.7 %add_bitcast_fusion.maps_in = s32[8,128]{1,0:T(8,128)S(1)} fusion(s32[1024]{0:T(1024)} %param.6, s32[1024]{0:T(1024)} %param.7), kind=kLoop, calls=%fused_computation | loop fusion | flops 2048 | bytes 12288 | tf_op jit(solution)/shard_map/reshape | solution.py:607
  1.3 25.3 %shard_map.59 = (f32[8,5,8,128]{3,2,1,0:T(8,128)S(1)}, f32[5,32,136]{2,1,0:T(8,128)S(1)}) custom-call(f32[8,5,8,128]{3,2,1,0:T(8,128)} %boxes_in.1, f32[5,16,512]{2,1,0:T(8,128)} %coarse_in.1, s32[8,128]{1,0:T(8,128)S(1)} %add_bitcast_fusion.maps_in), custom_call_target="tpu_custom_call" | custom-call | tf_op jit(solution)/shard_map/pallas_call | solution.py:548
  26.6 0.7 %shard_map.60 = (f32[8,5,8,128]{3,2,1,0:T(8,128)}, f32[5,32,136]{2,1,0:T(8,128)}) custom-call(f32[8,5,8,128]{3,2,1,0:T(8,128)S(1)} %get-tuple-element.6.fine_in, f32[5,32,136]{2,1,0:T(8,128)S(1)} %get-tuple-element.7.reflux_in), custom_call_target="tpu_custom_call" | custom-call | tf_op jit(solution)/shard_map/pallas_call | solution.py:609
